TPU v7x, 32 devices: a whole 2x2x4 slice. The times are simulated.
32 devices in a mesh: edges: 32 (over z, y, x, core).
Axes of the slice: x: 2, y: 2, z: 4, core: 2. Of those that a mesh axis runs over, the one named last changes fastest.
Arguments:
- messages: float32 [12288, 512], P('edges'), may hold values from -6 to 6
- rev_slot: int32 [12288], P('edges'), may hold values from 0 to 95
- tri_basis: float32 [16, 49152], P(None, 'edges'), may hold values from -6 to 6
- tri_source: int32 [49152], P('edges'), may hold values from 0 to 575
- tri_target: int32 [49152], P('edges'), may hold values from 0 to 127
- tile_block: int32 [384], P('edges'), may hold values from 0 to 2
- tile_count: int32 [32], P('edges'), may hold values from 6 to 12, as said below
- w_basis: float32 [16, 512], replicated, may hold values from -1.5 to 1.5
- w_rev: float32 [512, 512], replicated, may hold values from -0.25 to 0.25
- w_layers: float32 [2, 512, 512], replicated, may hold values from -0.25 to 0.25
- cotangent: float32 [12288, 512], P('edges'), may hold values from -6 to 6
Outputs:
- out_messages: float32 [12288, 512], P('edges')
- grad_messages: float32 [12288, 512], P('edges')
- grad_layers: float32 [2, 262144], P(None, 'edges')
- grad_rev: float32 [262144], P('edges')
- grad_basis: float32 [16, 512], replicated
Inputs may be any that keep to these rules, and one draw needn't show every extreme that they name: Tiles j >= tile_count[d] of device d are ignored whatever they hold; some device has 12 live tiles.
All inputs are finite; a program needn't handle non-finite values.
Results may differ from a plain program's by a relative error of at most 0.0003.
Values sent between devices are 32-bit elements; how exact they have to be, the bound alone decides.
A program may use at most 64 MiB of HBM per device.

v0:
```python
import jax
import jax.numpy as jnp
from jax import lax
from jax.sharding import PartitionSpec as P


def partner(value, axis, bit):
    mask = 2**bit
    pairs = [(source, source ^ mask) for source in range(lax.axis_size(axis))]
    return lax.ppermute(value, axis, pairs)


def padded(block, sides, width):
    for axis, dim in sides:
        count = lax.axis_size(axis)
        forward = [(i, i + 1) for i in range(count - 1)]
        forward.append((count - 1, 0))
        backward = [(target, source) for source, target in forward]
        low = lax.ppermute(
            lax.slice_in_dim(block, block.shape[dim] - width, None, axis=dim), axis, forward
        )
        high = lax.ppermute(lax.slice_in_dim(block, 0, width, axis=dim), axis, backward)
        block = jnp.concatenate([low, block, high], axis=dim)
    return block


def from_behind(block, axis, distance):
    devices = range(lax.axis_size(axis))
    route = [((i - distance) % len(devices), i) for i in devices]
    return lax.ppermute(block, axis, route)


def full_dot(left, right):
    return jnp.dot(left, right, precision=lax.Precision.HIGHEST, preferred_element_type=jnp.float32)


def lead_dot(left, right):
    return lax.dot_general(
        left,
        right,
        (((0,), (0,)), ((), ())),
        precision=lax.Precision.HIGHEST,
        preferred_element_type=jnp.float32,
    )


def trail_dot(left, right):
    return lax.dot_general(
        left,
        right,
        (((1,), (1,)), ((), ())),
        precision=lax.Precision.HIGHEST,
        preferred_element_type=jnp.float32,
    )


def silu_slope(values):
    sigma = jax.nn.sigmoid(values)
    return sigma * (1.0 + values * (1.0 - sigma))


def partner_rows(edge_rows, rev_slot):
    group = edge_rows.shape[0] // 4
    levels = lax.axis_size("edges").bit_length() - 1
    bit_list = [0, levels // 3, 2 * levels // 3, levels - 1]
    pieces = []
    for group_id in range(4):
        arrived = partner(
            edge_rows[group_id * group : (group_id + 1) * group], "edges", bit_list[group_id]
        )
        pieces.append(
            jnp.take(arrived, rev_slot[group_id * group : (group_id + 1) * group], axis=0)
        )
    return jnp.concatenate(pieces, axis=0)


def on_device(
    messages,
    rev_slot,
    tri_basis,
    tri_source,
    tri_target,
    tile_block,
    tile_count,
    w_basis,
    w_rev,
    w_layers,
    cotangent,
):
    edges_dev = messages.shape[0]
    width = messages.shape[1]
    halo_rows = edges_dev // 4
    depth = w_layers.shape[0]
    scale = float(edges_dev * lax.axis_size("edges")) ** (-0.5)
    live_count = tile_count[0]
    window = padded(messages, (("edges", 0),), halo_rows)
    columns_id = jnp.arange(128, dtype=jnp.int32)

    def tile_inputs(tile):
        first = tile * 128
        source = lax.dynamic_slice_in_dim(tri_source, first, 128)
        target = lax.dynamic_slice_in_dim(tri_target, first, 128)
        coeffs = lax.dynamic_slice_in_dim(tri_basis, first, 128, 1)
        gathered = jnp.take(window, source, axis=0)
        tri_weight = lead_dot(coeffs, w_basis)
        onehot = (target[:, None] == columns_id[None, :]).astype(jnp.float32)
        block_start = tile_block[tile] * 128
        return (source, coeffs, gathered, tri_weight, onehot, block_start)

    def forward_tile(tile, agg):
        source, coeffs, gathered, tri_weight, onehot, block_start = tile_inputs(tile)
        contrib = lead_dot(onehot, gathered * tri_weight)
        current = lax.dynamic_slice_in_dim(agg, block_start, 128)
        return lax.dynamic_update_slice_in_dim(agg, current + contrib, block_start, 0)

    agg = lax.fori_loop(0, live_count, forward_tile, jnp.zeros((edges_dev, width), jnp.float32))
    rev_proj = partner_rows(full_dot(messages, w_rev), rev_slot)
    gate_vals = jax.nn.silu(rev_proj)
    hidden = messages + agg + messages * gate_vals
    states = [hidden]
    pre_list = []
    for layer in range(depth):
        pre_act = full_dot(hidden, w_layers[layer])
        pre_list.append(pre_act)
        hidden = hidden + jax.nn.silu(pre_act)
        states.append(hidden)
    grad = cotangent
    local_terms = [None] * depth
    for layer in range(depth - 1, -1, -1):
        grad_pre = grad * silu_slope(pre_list[layer])
        local_terms[layer] = lead_dot(states[layer], grad_pre) * scale
        grad = grad + trail_dot(grad_pre, w_layers[layer])
    grad_agg = grad
    grad_msg = grad * (1.0 + gate_vals)
    grad_rev_proj = grad * messages * silu_slope(rev_proj)
    returned = partner_rows(grad_rev_proj, rev_slot)
    grad_msg = grad_msg + trail_dot(returned, w_rev)
    rev_term = lead_dot(messages, returned) * scale
    grad_stack = jnp.stack(local_terms + [rev_term]).reshape(depth + 1, width * width)
    shares = lax.psum_scatter(grad_stack, "edges", scatter_dimension=1, tiled=True)
    grad_layers = shares[:depth]
    grad_rev = shares[depth]

    def backward_tile(tile, carry):
        window_grad, basis_grad = carry
        source, coeffs, gathered, tri_weight, onehot, block_start = tile_inputs(tile)
        grad_block = lax.dynamic_slice_in_dim(grad_agg, block_start, 128)
        grad_prod = full_dot(onehot, grad_block)
        basis_grad = basis_grad + full_dot(coeffs, grad_prod * gathered)
        window_grad = window_grad.at[source].add(grad_prod * tri_weight)
        return (window_grad, basis_grad)

    start_carry = (
        jnp.zeros((edges_dev + 2 * halo_rows, width), jnp.float32),
        jnp.zeros(w_basis.shape, jnp.float32),
    )
    window_grad, basis_grad = lax.fori_loop(0, live_count, backward_tile, start_carry)
    from_next = from_behind(window_grad[:halo_rows], "edges", -1)
    from_prev = from_behind(window_grad[halo_rows + edges_dev :], "edges", 1)
    grad_msg = grad_msg + window_grad[halo_rows : halo_rows + edges_dev]
    grad_msg = grad_msg.at[edges_dev - halo_rows :].add(from_next)
    grad_msg = grad_msg.at[:halo_rows].add(from_prev)
    grad_basis = lax.psum(basis_grad * scale, "edges")
    return (hidden, grad_msg, grad_layers, grad_rev, grad_basis)


def solution(mesh):
    in_specs = (
        P("edges", None),
        P("edges"),
        P(None, "edges"),
        P("edges"),
        P("edges"),
        P("edges"),
        P("edges"),
        P(),
        P(),
        P(),
        P("edges", None),
    )
    out_specs = (P("edges", None), P("edges", None), P(None, "edges"), P("edges"), P())
    return jax.shard_map(
        on_device, mesh=mesh, in_specs=in_specs, out_specs=out_specs, check_vma=False
    )
```

profile of v0, /device:TPU:0, one launch (start us, length us, event | category | flops | bytes accessed | tf_op | source)
XLA Modules:
  0.0 376.4 jit_solution(1496146347250534961)
XLA Ops:
  9.1 6.4 %collective-permute-start.1 = (f32[96,512]{1,0:T(8,128)}, f32[96,512]{1,0:T(8,128)S(1)}, u32[]{:S(2)}, u32[]{:S(2)}) collective-permute-start(f32[96,512]{1,0:T(8,128)} %get-tuple-element.259), channel_id=1, source_target_pairs={{1,0},{2,1},{3,2},{4,3},{5,4},{6,5},{7,6},{8,7},{9,8},{10,9},{11,1... | collective-permute-start | bytes 589832 | tf_op jit(solution)/shard_map/ppermute | solution.py:22
  19.0 5.3 %collective-permute-done = f32[96,512]{1,0:T(8,128)S(1)} collective-permute-done((f32[96,512]{1,0:T(8,128)S(1)}, f32[96,512]{1,0:T(8,128)S(1)}, u32[]{:S(2)}, u32[]{:S(2)}) %collective-permute-start) | collective-permute-done | bytes 196640 | tf_op jit(solution)/shard_map/ppermute | solution.py:19
  27.0 52.6 %while.26 = (s32[]{:T(128)}, f32[384,512]{1,0:T(8,128)}, s32[]{:T(128)}, s32[12]{0:T(128)S(1)}, s32[1536]{0:T(1024)}, /*index=5*/s32[1536]{0:T(1024)}, f32[576,5...) while((s32[]{:T(128)}, f32[384,512]{1,0:T(8,128)}, ...), condition=%wide.region_1.3_spmd.clone, body=%wide.region_0.2_spmd.clone.sunk | while | flops 113461008 | bytes 1884215 | solution.py:116
  39.7 2.0 fusion.64
  47.1 2.0 fusion.64
  54.5 2.0 fusion.64
  79.6 2.4 gather_fusion.2
  83.0 2.5 gather_fusion.5
  90.2 2.4 gather_fusion.3
  97.1 2.8 multiply_add_fusion
  101.6 2.2 fusion.20
  103.9 2.1 copy.21
  106.0 2.8 multiply_multiply_fusion
  109.6 18.3 %collective-permute-start.6 = (f32[96,512]{1,0:T(8,128)S(1)}, f32[96,512]{1,0:T(8,128)}, u32[]{:S(2)}, u32[]{:S(2)}) collective-permute-start(f32[96,512]{1,0:T(8,128)S(1)} %get-tuple-element.251), channel_id=1, source_target_pairs={{0,1},{1,0},{2,3},{3,2},{4,5},{5,4},{6,7},{7,6},{8,9},{9,8},{10,11... | collective-permute-start | bytes 589832 | tf_op jit(solution)/shard_map/ppermute | solution.py:10
  127.8 2.3 fusion.21
  132.2 8.2 %collective-permute-start.9 = (f32[96,512]{1,0:T(8,128)}, f32[96,512]{1,0:T(8,128)}, u32[]{:S(2)}, u32[]{:S(2)}) collective-permute-start(f32[96,512]{1,0:T(8,128)} %get-tuple-element.252), channel_id=1, source_target_pairs={{0,16},{1,17},{2,18},{3,19},{4,20},{5,21},{6,22},{7,23},{8,24},{9,... | collective-permute-start | bytes 589832 | tf_op jit(solution)/shard_map/ppermute | solution.py:10
  140.4 7.9 %collective-permute-start.8 = (f32[96,512]{1,0:T(8,128)}, f32[96,512]{1,0:T(8,128)S(1)}, u32[]{:S(2)}, u32[]{:S(2)}) collective-permute-start(f32[96,512]{1,0:T(8,128)} %get-tuple-element.253), channel_id=1, source_target_pairs={{0,8},{1,9},{2,10},{3,11},{4,12},{5,13},{6,14},{7,15},{8,0},{9,1},... | collective-permute-start | bytes 589832 | tf_op jit(solution)/shard_map/ppermute | solution.py:10
  148.3 2.4 gather_fusion.6
  152.4 2.4 gather_fusion.9
  162.7 3.9 %fusion.19 = f32[512,512]{0,1:T(8,128)} fusion(f32[384,512]{1,0:T(8,128)S(1)} %copy-done.1, f32[96,512]{1,0:T(8,128)} %broadcast_select_fusion, f32[96,512]{1,0:T(8,128)} %broadcast_select_fusion.1, f32[96,512]{1,0:T(8,128)S(1)} %broadcast_select_fusion.2, f32[96,512]{1,0:T(8,128)S(1)} %copy-done.9), kind=kOutput, calls=%fused_computation.43 | convolution fusion | flops 1208811520 | bytes 2621440 | tf_op jit(solution)/shard_map/dot_general | solution.py:38
  169.6 4.3 %pad_maximum_fusion = f32[3,262144]{1,0:T(4,128)} fusion(f32[1,262144]{1,0:T(1,128)S(1)} %bitcast.54, f32[1,262144]{1,0:T(1,128)S(1)} %bitcast.52, f32[1,262144]{1,0:T(1,128)S(1)} %bitcast.53), kind=kLoop, calls=%fused_computation.41 | loop fusion | flops 1572864 | bytes 6291456 | tf_op jit(solution)/shard_map/stack | solution.py:139
  174.1 81.6 %while.27 = (s32[]{:T(128)}, f32[576,512]{1,0:T(8,128)S(1)}, f32[16,512]{1,0:T(8,128)S(1)}, s32[]{:T(128)}, s32[1536]{0:T(1024)}, /*index=5*/s32[1536]{0:T(1024)...) while((s32[]{:T(128)}, f32[576,512]{1,0:T(8,128)S(1)}, ...), condition=%wide.region_4.7_spmd.clone, body=%wide.region_2.6_spmd.clone.sunk | while | flops 126117648 | bytes 3007051 | solution.py:157
  183.4 2.2 scatter_fusion
  195.0 2.2 scatter_fusion
  206.6 2.2 scatter_fusion
  218.1 2.3 scatter_fusion
  229.7 2.2 scatter_fusion
  241.3 2.2 scatter_fusion
  252.9 2.2 scatter_fusion
  256.4 34.9 %collective-permute-start.11 = (f32[96,512]{1,0:T(8,128)S(1)}, f32[96,512]{1,0:T(8,128)S(1)}, u32[]{:S(2)}, u32[]{:S(2)}) collective-permute-start(f32[96,512]{1,0:T(8,128)S(1)} %get-tuple-element.249), channel_id=1, source_target_pairs={{31,0},{0,1},{1,2},{2,3},{3,4},{4,5},{5,6},{6,7},{7,8},{8,9},{9,10... | collective-permute-start | bytes 589832 | tf_op jit(solution)/shard_map/ppermute | solution.py:30
  291.3 70.5 %psum.7 = f32[16,512]{1,0:T(8,128)} all-reduce(f32[16,512]{1,0:T(8,128)S(1)} %broadcast_multiply_fusion), channel_id=1, replica_groups=mesh['edges'=32] {'edges'}, use_global_device_ids=true, to_apply=%region_6.9 | all-reduce | flops 8192 | bytes 65536 | tf_op jit(solution)/shard_map/psum | solution.py:163
  361.8 3.3 fusion.22
  (195 shorter events, 133.0 us)
Async XLA Ops:
  7.2 8.3 %copy-start = (f32[512,512]{1,0:T(8,128)S(1)}, f32[512,512]{1,0:T(8,128)}, u32[]{:S(2)}) copy-start(f32[512,512]{1,0:T(8,128)} %param.31) | copy-start | bytes 3145732
  7.2 8.3 %copy-start.1 = (f32[384,512]{1,0:T(8,128)S(1)}, f32[384,512]{1,0:T(8,128)}, u32[]{:S(2)}) copy-start(f32[384,512]{1,0:T(8,128)} %param.23) | copy-start | bytes 2359300
  7.2 359.0 %all-reduce.3.cloned.1.call-start = ((), (), s32[]{:S(2)}) async-start(), calls=%async_computation | async-start | bytes 8388608
  9.1 16.9 %collective-permute-start.1 = (f32[96,512]{1,0:T(8,128)}, f32[96,512]{1,0:T(8,128)S(1)}, u32[]{:S(2)}, u32[]{:S(2)}) collective-permute-start(f32[96,512]{1,0:T(8,128)} %get-tuple-element.259), channel_id=1, source_target_pairs={{1,0},{2,1},{3,2},{4,3},{5,4},{6,5},{7,6},{8,7},{9,8},{10,9},{11,1... | collective-permute-start | bytes 589832 | tf_op jit(solution)/shard_map/ppermute | solution.py:22
  15.5 8.8 %collective-permute-start = (f32[96,512]{1,0:T(8,128)S(1)}, f32[96,512]{1,0:T(8,128)S(1)}, u32[]{:S(2)}, u32[]{:S(2)}) collective-permute-start(f32[96,512]{1,0:T(8,128)S(1)} %get-tuple-element.260), channel_id=1, source_target_pairs={{0,1},{1,2},{2,3},{3,4},{4,5},{5,6},{6,7},{7,8},{8,9},{9,10},{10,1... | collective-permute-start | bytes 589832 | tf_op jit(solution)/shard_map/ppermute | solution.py:19
  16.9 1.9 copy-start.14
  17.8 61.7 %collective-permute-start.2 = (f32[96,512]{1,0:T(8,128)}, f32[96,512]{1,0:T(8,128)}, u32[]{:S(2)}, u32[]{:S(2)}) collective-permute-start(f32[96,512]{1,0:T(8,128)} %get-tuple-element.255), channel_id=1, source_target_pairs={{0,1},{1,0},{2,3},{3,2},{4,5},{5,4},{6,7},{7,6},{8,9},{9,8},{10,11... | collective-permute-start | bytes 589832 | tf_op jit(solution)/shard_map/ppermute | solution.py:10
  17.8 65.2 %collective-permute-start.5 = (f32[96,512]{1,0:T(8,128)}, f32[96,512]{1,0:T(8,128)}, u32[]{:S(2)}, u32[]{:S(2)}) collective-permute-start(f32[96,512]{1,0:T(8,128)} %get-tuple-element.256), channel_id=1, source_target_pairs={{0,16},{1,17},{2,18},{3,19},{4,20},{5,21},{6,22},{7,23},{8,24},{9,... | collective-permute-start | bytes 589832 | tf_op jit(solution)/shard_map/ppermute | solution.py:10
  17.8 69.3 %collective-permute-start.4 = (f32[96,512]{1,0:T(8,128)}, f32[96,512]{1,0:T(8,128)S(1)}, u32[]{:S(2)}, u32[]{:S(2)}) collective-permute-start(f32[96,512]{1,0:T(8,128)} %get-tuple-element.257), channel_id=1, source_target_pairs={{0,8},{1,9},{2,10},{3,11},{4,12},{5,13},{6,14},{7,15},{8,0},{9,1},... | collective-permute-start | bytes 589832 | tf_op jit(solution)/shard_map/ppermute | solution.py:10
  24.2 0.7 copy-start.12
  24.9 65.3 %collective-permute-start.3 = (f32[96,512]{1,0:T(8,128)}, f32[96,512]{1,0:T(8,128)}, u32[]{:S(2)}, u32[]{:S(2)}) collective-permute-start(f32[96,512]{1,0:T(8,128)} %get-tuple-element.258), channel_id=1, source_target_pairs={{0,2},{1,3},{2,0},{3,1},{4,6},{5,7},{6,4},{7,5},{8,10},{9,11},{10,... | collective-permute-start | bytes 589832 | tf_op jit(solution)/shard_map/ppermute | solution.py:10
  25.9 1.1 copy-start.4
  25.9 1.1 copy-start.16
  83.0 23.0 %copy-start.5 = (f32[96,512]{1,0:T(8,128)}, f32[96,512]{1,0:T(8,128)S(1)}, u32[]{:S(2)}) copy-start(f32[96,512]{1,0:T(8,128)S(1)} %broadcast_select_fusion.7) | copy-start | bytes 589828
  90.2 3.5 copy-start.6
  93.7 12.3 %copy-start.8 = (f32[96,512]{1,0:T(8,128)}, f32[96,512]{1,0:T(8,128)S(1)}, u32[]{:S(2)}) copy-start(f32[96,512]{1,0:T(8,128)S(1)} %broadcast_select_fusion.6) | copy-start | bytes 589828
  93.7 2.0 copy-start.11
  97.1 2.8 copy-start.15
  103.9 2.1 copy-start.7
  109.6 38.7 %collective-permute-start.6 = (f32[96,512]{1,0:T(8,128)S(1)}, f32[96,512]{1,0:T(8,128)}, u32[]{:S(2)}, u32[]{:S(2)}) collective-permute-start(f32[96,512]{1,0:T(8,128)S(1)} %get-tuple-element.251), channel_id=1, source_target_pairs={{0,1},{1,0},{2,3},{3,2},{4,5},{5,4},{6,7},{7,6},{8,9},{9,8},{10,11... | collective-permute-start | bytes 589832 | tf_op jit(solution)/shard_map/ppermute | solution.py:10
  132.2 20.2 %collective-permute-start.9 = (f32[96,512]{1,0:T(8,128)}, f32[96,512]{1,0:T(8,128)}, u32[]{:S(2)}, u32[]{:S(2)}) collective-permute-start(f32[96,512]{1,0:T(8,128)} %get-tuple-element.252), channel_id=1, source_target_pairs={{0,16},{1,17},{2,18},{3,19},{4,20},{5,21},{6,22},{7,23},{8,24},{9,... | collective-permute-start | bytes 589832 | tf_op jit(solution)/shard_map/ppermute | solution.py:10
  140.4 16.1 %collective-permute-start.8 = (f32[96,512]{1,0:T(8,128)}, f32[96,512]{1,0:T(8,128)S(1)}, u32[]{:S(2)}, u32[]{:S(2)}) collective-permute-start(f32[96,512]{1,0:T(8,128)} %get-tuple-element.253), channel_id=1, source_target_pairs={{0,8},{1,9},{2,10},{3,11},{4,12},{5,13},{6,14},{7,15},{8,0},{9,1},... | collective-permute-start | bytes 589832 | tf_op jit(solution)/shard_map/ppermute | solution.py:10
  148.3 11.3 %collective-permute-start.7 = (f32[96,512]{1,0:T(8,128)}, f32[96,512]{1,0:T(8,128)S(1)}, u32[]{:S(2)}, u32[]{:S(2)}) collective-permute-start(f32[96,512]{1,0:T(8,128)} %get-tuple-element.254), channel_id=1, source_target_pairs={{0,2},{1,3},{2,0},{3,1},{4,6},{5,7},{6,4},{7,5},{8,10},{9,11},{10,... | collective-permute-start | bytes 589832 | tf_op jit(solution)/shard_map/ppermute | solution.py:10
  159.6 3.1 copy-start.9
  162.0 0.7 copy-start.10
  168.1 1.2 copy-start.2
  168.1 1.5 copy-start.3
  256.4 109.7 %collective-permute-start.11 = (f32[96,512]{1,0:T(8,128)S(1)}, f32[96,512]{1,0:T(8,128)S(1)}, u32[]{:S(2)}, u32[]{:S(2)}) collective-permute-start(f32[96,512]{1,0:T(8,128)S(1)} %get-tuple-element.249), channel_id=1, source_target_pairs={{31,0},{0,1},{1,2},{2,3},{3,4},{4,5},{5,6},{6,7},{7,8},{8,9},{9,10... | collective-permute-start | bytes 589832 | tf_op jit(solution)/shard_map/ppermute | solution.py:30
  291.3 73.8 %collective-permute-start.10 = (f32[96,512]{1,0:T(8,128)}, f32[96,512]{1,0:T(8,128)}, u32[]{:S(2)}, u32[]{:S(2)}) collective-permute-start(f32[96,512]{1,0:T(8,128)} %get-tuple-element.250), channel_id=1, source_target_pairs={{1,0},{2,1},{3,2},{4,3},{5,4},{6,5},{7,6},{8,7},{9,8},{10,9},{11,1... | collective-permute-start | bytes 589832 | tf_op jit(solution)/shard_map/ppermute | solution.py:30
  366.1 3.4 copy-start.13
Sparse Core Ops, SparseCore 0:
  174.1 149.8 all-reduce.2
where the time goes:
time: 381 us; the launch traced here: 376 us
  starting transfers between devices  76.7 us (20%)
  matrix products  75 us (20%)
  blocking collectives  70.5 us (19%)
  local copies, waits for them, and re-layouts  69.4 us (18%)
  other arithmetic  44.7 us (12%)
  loops' own time  20.3 us (5%)
  between operations  14.4 us (4%)
  waiting for transfers between devices  5.33 us (1%)
    psum x1, blocking collectives, on_device(): grad_basis = lax.psum(basis_grad * scale, 'edges')  70.5 us
    dot_general x24, matrix products, lead_dot(): lax.dot_general(left, right, (((0,), (0,)), ((), ())), precision=lax.Prec...  43.5 us
    ppermute x8, starting transfers between devices, partner(): return lax.ppermute(value, axis, pairs)  35.4 us
    ppermute x2, starting transfers between devices, from_behind(): return lax.ppermute(block, axis, route)  34.9 us
    dot_general x17, matrix products, full_dot(): jnp.dot(left, right, precision=lax.Precision.HIGHEST, preferred_element_t...  23.7 us
    gather x8, local copies, waits for them, and re-layouts, partner_rows(): jnp.take(arrived, rev_slot[group_id * group:(group_id + 1) * group], axis=0)  16.2 us
    gather x14, local copies, waits for them, and re-layouts, tile_inputs(): gathered = jnp.take(window, source, axis=0)  15.5 us
    scatter-add x7, other arithmetic, backward_tile(): window_grad = window_grad.at[source].add(grad_prod * tri_weight)  15.5 us
  transfers between devices with their start and end apart: 13, of which 1 were waited for; matrix products, arithmetic and copies ran while one was open for 40% of the time, Pallas kernels for 0%

commit v1 on v0

v1 whole, which is shorter than its diff:
```python
import jax
import jax.numpy as jnp
from jax import lax
from jax.experimental import pallas as pl
from jax.experimental.pallas import tpu as pltpu
from jax.sharding import PartitionSpec as P

F32 = jnp.float32
BF16 = jnp.bfloat16
VMEM_LIMIT = 48 * 1024 * 1024


def split(value):
    high = value.astype(BF16)
    low = (value - high.astype(F32)).astype(BF16)
    return high, low


def dot(left, right, dims=((1,), (0,))):
    return lax.dot_general(left, right, (dims, ((), ())), preferred_element_type=F32)


def dot3(left, right, dims=((1,), (0,))):
    (lh, ll), (rh, rl) = left, right
    return dot(lh, rh, dims) + dot(lh, rl, dims) + dot(ll, rh, dims)


def pick(onehot, value):
    high, low = split(value)
    return dot(onehot, high) + dot(onehot, low)


def onehot_rows(column, width):
    ids = lax.broadcasted_iota(jnp.int32, (column.shape[0], width), 1)
    return jnp.where(column == ids, 1.0, 0.0).astype(BF16)


def onehot_columns(row, height):
    ids = lax.broadcasted_iota(jnp.int32, (height, row.shape[1]), 0)
    return jnp.where(row == ids, 1.0, 0.0).astype(BF16)


def silu_pair(values):
    sigma = jax.nn.sigmoid(values)
    return values * sigma, sigma * (1.0 + values * (1.0 - sigma))


def triplet_weight(basis, w_basis):
    bh, bl = split(basis)
    wh, wl = split(w_basis)
    return dot(
        jnp.concatenate([bh, bl, bh], axis=0),
        jnp.concatenate([wh, wh, wl], axis=0),
        ((0,), (0,)),
    )


def gather_window(low, messages, high, src_col):
    window = jnp.concatenate([low[...], messages[...], high[...]], axis=0)
    return pick(onehot_rows(src_col[...], window.shape[0]), window)


def agg_kernel(low, messages, high, src_col, tgt_row, basis, w_basis, agg):
    gathered = gather_window(low, messages, high, src_col)
    terms = gathered * triplet_weight(basis[...], w_basis[...])
    agg[...] = pick(onehot_columns(tgt_row[...], messages.shape[0]), terms)


def mlp_kernel(
    scale,
    messages,
    agg,
    r0,
    r1,
    r2,
    r3,
    slot_col,
    w_rev,
    w_layers,
    cotangent,
    out,
    grad0,
    grad_msg,
    grad_rev_proj,
    weight_grads,
):
    depth = w_layers.shape[0]
    group = r0.shape[0]
    highs, lows = [], []
    for k, arrived in enumerate((r0, r1, r2, r3)):
        onehot = onehot_rows(slot_col[k * group : (k + 1) * group, :], group)
        ah, al = split(arrived[...])
        highs.append(dot(onehot, ah).astype(BF16))
        lows.append(dot(onehot, al).astype(BF16))
    rev = (jnp.concatenate(highs, axis=0), jnp.concatenate(lows, axis=0))
    gate, rev_slope = silu_pair(dot3(rev, split(w_rev[...])))
    msg = messages[...]
    hidden = msg + agg[...] + msg * gate
    states, slopes, weights = [], [], []
    for layer in range(depth):
        state, weight = split(hidden), split(w_layers[layer])
        act, slope = silu_pair(dot3(state, weight))
        hidden = hidden + act
        states.append(state)
        slopes.append(slope)
        weights.append(weight)
    out[...] = hidden
    grad = cotangent[...]
    for layer in range(depth - 1, -1, -1):
        grad_pre = split(grad * slopes[layer])
        weight_grads[layer] = dot3(states[layer], grad_pre, ((0,), (0,))) * scale
        grad = grad + dot3(grad_pre, weights[layer], ((1,), (1,)))
    grad0[...] = grad
    grad_msg[...] = grad * (1.0 + gate)
    g_rev = grad * msg * rev_slope
    grad_rev_proj[...] = g_rev
    weight_grads[depth] = dot3(rev, split(g_rev), ((0,), (0,))) * scale


def back_kernel(
    scale,
    low,
    messages,
    high,
    src_col,
    src_row,
    tgt_col,
    basis,
    w_basis,
    grad0,
    window_grad,
    basis_grad,
):
    gathered = gather_window(low, messages, high, src_col)
    grad_prod = pick(onehot_rows(tgt_col[...], grad0.shape[0]), grad0[...])
    basis_grad[...] = dot3(split(basis[...]), split(grad_prod * gathered)) * scale
    terms = grad_prod * triplet_weight(basis[...], w_basis[...])
    window_grad[...] = pick(onehot_columns(src_row[...], window_grad.shape[0]), terms)


def end_kernel(
    grad_msg, window_grad, from_next, from_prev, b0, b1, b2, b3, slot_col, w_rev, out
):
    group = b0.shape[0]
    edges = out.shape[0]
    highs, lows = [], []
    for k, arrived in enumerate((b0, b1, b2, b3)):
        onehot = onehot_rows(slot_col[k * group : (k + 1) * group, :], group)
        ah, al = split(arrived[...])
        highs.append(dot(onehot, ah).astype(BF16))
        lows.append(dot(onehot, al).astype(BF16))
    returned = (jnp.concatenate(highs, axis=0), jnp.concatenate(lows, axis=0))
    out[...] = (
        grad_msg[...]
        + window_grad[group : group + edges, :]
        + dot3(returned, split(w_rev[...]), ((1,), (1,)))
    )
    out[:group, :] = out[:group, :] + from_prev[...]
    out[edges - group :, :] = out[edges - group :, :] + from_next[...]


def call(kernel, name, shapes, flops, *args):
    specs = [pl.BlockSpec(memory_space=pltpu.VMEM)]
    return pl.pallas_call(
        kernel,
        out_shape=[jax.ShapeDtypeStruct(shape, F32) for shape in shapes],
        in_specs=specs * len(args),
        out_specs=specs * len(shapes),
        cost_estimate=pl.CostEstimate(
            flops=flops, bytes_accessed=4 * 1024 * 1024, transcendentals=0
        ),
        compiler_params=pltpu.CompilerParams(vmem_limit_bytes=VMEM_LIMIT),
        name=name,
    )(*args)


def shift(block, distance):
    count = lax.axis_size("edges")
    return lax.ppermute(block, "edges", [(i, (i + distance) % count) for i in range(count)])


def exchange(rows):
    group = rows.shape[0] // 4
    count = lax.axis_size("edges")
    levels = count.bit_length() - 1
    arrived = []
    for k, bit in enumerate((0, levels // 3, 2 * levels // 3, levels - 1)):
        pairs = [(i, i ^ (1 << bit)) for i in range(count)]
        arrived.append(lax.ppermute(rows[k * group : (k + 1) * group], "edges", pairs))
    return arrived


def on_device(
    messages,
    rev_slot,
    tri_basis,
    tri_source,
    tri_target,
    tile_block,
    tile_count,
    w_basis,
    w_rev,
    w_layers,
    cotangent,
):
    edges, width = messages.shape
    halo = edges // 4
    depth = w_layers.shape[0]
    tiles = tile_block.shape[0]
    slots = tri_source.shape[0]
    scale = float(edges * lax.axis_size("edges")) ** (-0.5)
    low = shift(messages[edges - halo :], 1)
    high = shift(messages[:halo], -1)
    arrived = exchange(messages)

    live = jnp.arange(tiles, dtype=jnp.int32) < tile_count[0]
    target = tile_block[:, None] * 128 + tri_target.reshape(tiles, 128)
    target = jnp.where(live[:, None], target, -1)
    tgt_row, tgt_col = target.reshape(1, slots), target.reshape(slots, 1)
    src_row, src_col = tri_source.reshape(1, slots), tri_source.reshape(slots, 1)
    slot_col = rev_slot.reshape(edges, 1)

    (agg,) = call(
        agg_kernel,
        "agg",
        [(edges, width)],
        4 * slots * (2 * edges + 2 * halo) * width,
        low,
        messages,
        high,
        src_col,
        tgt_row,
        tri_basis,
        w_basis,
    )
    out, grad0, grad_msg, g_rev, weight_grads = call(
        lambda *refs: mlp_kernel(scale, *refs),
        "mlp",
        [(edges, width)] * 4 + [(depth + 1, width, width)],
        6 * 9 * edges * width * width,
        messages,
        agg,
        *arrived,
        slot_col,
        w_rev,
        w_layers,
        cotangent,
    )
    shares = lax.psum_scatter(weight_grads, "edges", scatter_dimension=1, tiled=True)
    shares = shares.reshape(depth + 1, -1)
    back = exchange(g_rev)
    window_grad, basis_grad = call(
        lambda *refs: back_kernel(scale, *refs),
        "back",
        [(edges + 2 * halo, width), w_basis.shape],
        4 * slots * (3 * edges + 4 * halo) * width,
        low,
        messages,
        high,
        src_col,
        src_row,
        tgt_col,
        tri_basis,
        w_basis,
        grad0,
    )
    from_next = shift(window_grad[:halo], -1)
    from_prev = shift(window_grad[halo + edges :], 1)
    grad_basis = lax.psum(basis_grad, "edges")
    (grad_out,) = call(
        end_kernel,
        "end",
        [(edges, width)],
        6 * edges * width * width,
        grad_msg,
        window_grad,
        from_next,
        from_prev,
        *back,
        slot_col,
        w_rev,
    )
    return (out, grad_out, shares[:depth], shares[depth], grad_basis)


def solution(mesh):
    in_specs = (
        P("edges", None),
        P("edges"),
        P(None, "edges"),
        P("edges"),
        P("edges"),
        P("edges"),
        P("edges"),
        P(),
        P(),
        P(),
        P("edges", None),
    )
    out_specs = (P("edges", None), P("edges", None), P(None, "edges"), P("edges"), P())
    return jax.shard_map(
        on_device, mesh=mesh, in_specs=in_specs, out_specs=out_specs, check_vma=False
    )
```

time: 381 us -> 192 us (0.50); the launches traced: 376 us -> 192 us
  waiting for transfers between devices: 5.33 us -> 84.7 us
  matrix products: 75 us -> 0 us
  starting transfers between devices: 76.7 us -> 11.4 us
  local copies, waits for them, and re-layouts: 69.4 us -> 11.7 us
  other arithmetic: 44.7 us -> 0.08 us
  blocking collectives: 70.5 us -> 42.9 us
  Pallas kernels: 0 us -> 25.9 us
  loops' own time: 20.3 us -> 0 us
    dot_general x44 -> x0, matrix products: 75 us -> none  [the longest x24 43.5 us: lead_dot(): lax.dot_general(left, right, (((0,), (0,)), ((), ())), precision=lax.Prec...]
    reduce_scatter x0 -> x1, waiting for transfers between devices: none -> 73.8 us  [on_device(): lax.psum_scatter(weight_grads, 'edges', scatter_dimension=1, tiled=True)]
    ppermute x12, starting transfers between devices: 76.7 us -> 11.4 us  [the longest x4 9.89 us: shift(): lax.ppermute(block, 'edges', [(i, (i + distance) % count) for i in range(...]
    gather x22 -> x0, local copies, waits for them, and re-layouts: 31.8 us -> none  [the longest x8 16.2 us: partner_rows(): jnp.take(arrived, rev_slot[group_id * group:(group_id + 1) * group], axis=0)]
    psum x1, blocking collectives: 70.5 us -> 42.9 us  [on_device(): grad_basis = lax.psum(basis_grad, 'edges')]
    pallas_call x0 -> x4, Pallas kernels: none -> 25.9 us  [call(): pl.pallas_call(kernel, out_shape=[jax.ShapeDtypeStruct(shape, F32) for sh...]
    another operation x2 -> x0, loops' own time: 20.3 us -> none  [the longest x1 10.2 us: on_device(): lax.fori_loop(0, live_count, forward_tile, jnp.zeros((edges_dev, width),...]
    dynamic_slice x28 -> x0, local copies, waits for them, and re-layouts: 18.9 us -> none  [the longest x14 10.7 us: tile_inputs(): target = lax.dynamic_slice_in_dim(tri_target, first, 128)]
  transfers between devices with their start and end apart: 13 -> 13, of which waited for: 1 -> 4; matrix products, arithmetic and copies ran while one was open for 40% -> 2% of each run, Pallas kernels for 0% -> 8%
where the time goes in v1:
time: 192 us
  waiting for transfers between devices  84.7 us (44%)
  blocking collectives  42.9 us (22%)
  Pallas kernels  25.9 us (13%)
  between operations  14.9 us (8%)
  local copies, waits for them, and re-layouts  11.7 us (6%)
  starting transfers between devices  11.4 us (6%)
    reduce_scatter x1, waiting for transfers between devices, on_device(): lax.psum_scatter(weight_grads, 'edges', scatter_dimension=1, tiled=True)  73.8 us
    psum x1, blocking collectives, on_device(): grad_basis = lax.psum(basis_grad, 'edges')  42.9 us
    pallas_call x4, Pallas kernels, call(): pl.pallas_call(kernel, out_shape=[jax.ShapeDtypeStruct(shape, F32) for sh...  25.9 us
    ppermute x4, starting transfers between devices, shift(): lax.ppermute(block, 'edges', [(i, (i + distance) % count) for i in range(...  9.89 us
    ppermute x4, waiting for transfers between devices, shift(): lax.ppermute(block, 'edges', [(i, (i + distance) % count) for i in range(...  9.41 us
    unnamed x34, local copies, waits for them, and re-layouts  7.4 us
  transfers between devices with their start and end apart: 13, of which 4 were waited for; matrix products, arithmetic and copies ran while one was open for 2% of the time, Pallas kernels for 8%

profile of v1, /device:TPU:0, one launch (start us, length us, event | category | flops | bytes accessed | tf_op | source)
XLA Modules:
  0.0 191.5 jit_solution(12709106663451489)
XLA Ops:
  7.2 0.0 reduce-scatter.2.cloned.1.call-start
  7.3 1.4 fusion.3
  8.6 6.4 %collective-permute-start.1 = (f32[96,512]{1,0:T(8,128)S(1)}, f32[96,512]{1,0:T(8,128)S(1)}, u32[]{:S(2)}, u32[]{:S(2)}) collective-permute-start(f32[96,512]{1,0:T(8,128)S(1)} %get-tuple-element.27), channel_id=1, source_target_pairs={{0,31},{1,0},{2,1},{3,2},{4,3},{5,4},{6,5},{7,6},{8,7},{9,8},{10,9... | collective-permute-start | bytes 589832 | tf_op jit(solution)/shard_map/ppermute | solution.py:179
  15.1 0.5 collective-permute-start
  15.6 1.0 reshape.57.src_col.refs_3_
  16.5 0.0 copy-start.2
  17.2 0.1 fusion
  17.3 0.1 reshape.58.refs_6_.slot_col
  17.4 6.5 %collective-permute-done.low.refs_0_ = f32[96,512]{1,0:T(8,128)S(1)} collective-permute-done((f32[96,512]{1,0:T(8,128)S(1)}, f32[96,512]{1,0:T(8,128)S(1)}, u32[]{:S(2)}, u32[]{:S(2)}) %collective-permute-start) | collective-permute-done | bytes 196640 | tf_op jit(solution)/shard_map/ppermute | solution.py:179
  24.0 4.4 %agg.1.refs_1_ = f32[384,512]{1,0:T(8,128)S(1)} custom-call(f32[96,512]{1,0:T(8,128)S(1)} %collective-permute-done.low.refs_0_, f32[384,512]{1,0:T(8,128)S(1)} %copy-done.1, f32[96,512]{1,0:T(8,128)S(1)} %collective-permute-done.1.high.refs_2_, s32[1536,1]{1,0:T(8,128)S(1)} %reshape.57.src_col.refs_3_, s32[1,1536]{1,0:T(1,128)S(1)} %select_n.13.tgt_row, ...), custom_call_target="tpu_custom_call" | custom-call | flops 3019898880 | bytes 4194304 | tf_op jit(solution)/shard_map/agg/pallas_call | solution.py:164
  28.5 1.4 collective-permute-done.4.refs_4_
  29.9 10.5 %mlp.1 = (f32[384,512]{1,0:T(8,128)}, f32[384,512]{1,0:T(8,128)S(1)}, f32[384,512]{1,0:T(8,128)S(1)}, f32[384,512]{1,0:T(8,128)S(1)}, f32[3,512,512]{2,1,0:T(8,128)}) custom-call(f32[384,512]{1,0:T(8,128)S(1)} %copy-done.1, f32[384,512]{1,0:T(8,128)S(1)} %agg.1.refs_1_, f32[96,512]{1,0:T(8,128)S(1)} %collective-permute-done.2.refs_2_, ...), custom_call_target="tpu_custom_call" | custom-call | flops 5435817984 | bytes 4194304 | tf_op jit(solution)/shard_map/mlp/pallas_call | solution.py:164
  40.4 0.9 copy-done.4
  41.3 0.9 copy-done.9
  42.2 0.0 reduce-scatter.2.cloned.1.call-update
  42.2 0.3 select_n.15.refs_5_
  42.5 0.4 copy-done.11
  42.9 1.1 copy-done.3
  44.0 1.1 copy-done.10
  45.2 7.7 %back.1 = (f32[576,512]{1,0:T(8,128)S(1)}, f32[16,512]{1,0:T(8,128)S(1)}) custom-call(f32[96,512]{1,0:T(8,128)S(1)} %collective-permute-done.low.refs_0_, f32[384,512]{1,0:T(8,128)S(1)} %copy-done.1, f32[96,512]{1,0:T(8,128)S(1)} %collective-permute-done.1.high.refs_2_, s32[1536,1]{1,0:T(8,128)S(1)} %copy-done.3, s32[1,1536]{1,0:T(1,128)S(1)} %reshape.56.refs_4_, ...), custom_call_target="tpu_custom_call" | custom-call | flops 4831838208 | bytes 4194304 | tf_op jit(solution)/shard_map/back/pallas_call | solution.py:164
  52.9 0.7 fusion.1
  53.6 3.0 %collective-permute-start.6 = (f32[96,512]{1,0:T(8,128)S(1)}, f32[96,512]{1,0:T(8,128)S(1)}, u32[]{:S(2)}, u32[]{:S(2)}) collective-permute-start(f32[96,512]{1,0:T(8,128)S(1)} %get-tuple-element.20), channel_id=1, source_target_pairs={{0,31},{1,0},{2,1},{3,2},{4,3},{5,4},{6,5},{7,6},{8,7},{9,8},{10,9... | collective-permute-start | bytes 589832 | tf_op jit(solution)/shard_map/ppermute | solution.py:179
  56.5 0.9 fusion.2
  57.4 1.5 collective-permute-start.11
  58.9 2.9 %collective-permute-done.6.from_next = f32[96,512]{1,0:T(8,128)S(1)} collective-permute-done((f32[96,512]{1,0:T(8,128)S(1)}, f32[96,512]{1,0:T(8,128)S(1)}, u32[]{:S(2)}, u32[]{:S(2)}) %collective-permute-start.6) | collective-permute-done | bytes 196640 | tf_op jit(solution)/shard_map/ppermute | solution.py:179
  61.8 42.9 %psum.7 = f32[16,512]{1,0:T(8,128)} all-reduce(f32[16,512]{1,0:T(8,128)S(1)} %get-tuple-element.18), channel_id=1, replica_groups=mesh['edges'=32] {'edges'}, use_global_device_ids=true, to_apply=%region_1.2 | all-reduce | flops 8192 | bytes 65536 | tf_op jit(solution)/shard_map/psum | solution.py:269
  104.7 3.3 %end.1 = f32[384,512]{1,0:T(8,128)} custom-call(f32[384,512]{1,0:T(8,128)S(1)} %get-tuple-element.13.grad_msg, f32[576,512]{1,0:T(8,128)S(1)} %get-tuple-element.15.window_grad, f32[96,512]{1,0:T(8,128)S(1)} %collective-permute-done.6.from_next, f32[96,512]{1,0:T(8,128)} %collective-permute-done.7.from_prev, f32[96,512]{1,0:T(8,128)} %collective-permute-done.8.b0, ...), custom_call_target="tpu_custom_call" | custom-call | flops 603979776 | bytes 4194304 | tf_op jit(solution)/shard_map/end/pallas_call | solution.py:164
  108.0 73.8 %reduce-scatter.2.cloned.1.call-done = f32[3,16,512]{2,1,0:T(8,128)} async-done(((f32[3,512,512]{2,1,0:T(8,128)}), f32[3,16,512]{2,1,0:T(8,128)}) %reduce-scatter.2.cloned.1.call-update) | async-done | bytes 98320 | tf_op jit(solution)/shard_map/reduce_scatter | solution.py:249
  181.8 0.8 slice_bitcast_fusion
  182.6 0.7 copy.21
  183.3 0.8 slice_bitcast_fusion.1
  184.1 0.6 copy.22
  (45 shorter events, 0.1 us)
Async XLA Ops:
  7.2 16.8 %copy-start.1 = (f32[384,512]{1,0:T(8,128)S(1)}, f32[384,512]{1,0:T(8,128)}, u32[]{:S(2)}) copy-start(f32[384,512]{1,0:T(8,128)} %refs_1_.1) | copy-start | bytes 2359300
  7.2 10.0 %copy-start.14 = (s32[12]{0:T(128)S(1)}, s32[12]{0:T(128)}, u32[]{:S(2)}) copy-start(s32[12]{0:T(128)} %param.16) | copy-start | bytes 148
  7.2 10.0 %copy-start.12 = (s32[1536]{0:T(1024)S(1)}, s32[1536]{0:T(1024)}, u32[]{:S(2)}) copy-start(s32[1536]{0:T(1024)} %param.15) | copy-start | bytes 18436
  7.2 10.1 %copy-start.13 = (s32[384]{0:T(512)S(1)}, s32[384]{0:T(512)}, u32[]{:S(2)}) copy-start(s32[384]{0:T(512)} %param.12) | copy-start | bytes 4612
  7.2 16.8 %copy-start.7 = (f32[16,1536]{1,0:T(8,128)S(1)}, f32[16,1536]{1,0:T(8,128)}, u32[]{:S(2)}) copy-start(f32[16,1536]{1,0:T(8,128)} %refs_6_.1) | copy-start | bytes 294916
  7.2 16.8 %copy-start.8 = (f32[16,512]{1,0:T(8,128)S(1)}, f32[16,512]{1,0:T(8,128)}, u32[]{:S(2)}) copy-start(f32[16,512]{1,0:T(8,128)} %refs_7_.3) | copy-start | bytes 98308
  7.2 174.6 %reduce-scatter.2.cloned.1.call-start = ((), (), s32[]{:S(2)}) async-start(), calls=%async_computation.1 | async-start | bytes 3244032 | tf_op jit(solution)/shard_map/reduce_scatter | solution.py:249
  8.6 15.4 %collective-permute-start.1 = (f32[96,512]{1,0:T(8,128)S(1)}, f32[96,512]{1,0:T(8,128)S(1)}, u32[]{:S(2)}, u32[]{:S(2)}) collective-permute-start(f32[96,512]{1,0:T(8,128)S(1)} %get-tuple-element.27), channel_id=1, source_target_pairs={{0,31},{1,0},{2,1},{3,2},{4,3},{5,4},{6,5},{7,6},{8,7},{9,8},{10,9... | collective-permute-start | bytes 589832 | tf_op jit(solution)/shard_map/ppermute | solution.py:179
  15.1 13.4 %collective-permute-start.2 = (f32[96,512]{1,0:T(8,128)S(1)}, f32[96,512]{1,0:T(8,128)S(1)}, u32[]{:S(2)}, u32[]{:S(2)}) collective-permute-start(f32[96,512]{1,0:T(8,128)S(1)} %get-tuple-element.27), channel_id=1, source_target_pairs={{0,1},{1,0},{2,3},{3,2},{4,5},{5,4},{6,7},{7,6},{8,9},{9,8},{10,11... | collective-permute-start | bytes 589832 | tf_op jit(solution)/shard_map/ppermute | solution.py:189
  15.1 8.9 %collective-permute-start = (f32[96,512]{1,0:T(8,128)S(1)}, f32[96,512]{1,0:T(8,128)S(1)}, u32[]{:S(2)}, u32[]{:S(2)}) collective-permute-start(f32[96,512]{1,0:T(8,128)S(1)} %get-tuple-element.28), channel_id=1, source_target_pairs={{0,1},{1,2},{2,3},{3,4},{4,5},{5,6},{6,7},{7,8},{8,9},{9,10},{10,1... | collective-permute-start | bytes 589832 | tf_op jit(solution)/shard_map/ppermute | solution.py:179
  15.6 12.9 %collective-permute-start.5 = (f32[96,512]{1,0:T(8,128)S(1)}, f32[96,512]{1,0:T(8,128)S(1)}, u32[]{:S(2)}, u32[]{:S(2)}) collective-permute-start(f32[96,512]{1,0:T(8,128)S(1)} %get-tuple-element.28), channel_id=1, source_target_pairs={{0,16},{1,17},{2,18},{3,19},{4,20},{5,21},{6,22},{7,23},{8,24},{9,... | collective-permute-start | bytes 589832 | tf_op jit(solution)/shard_map/ppermute | solution.py:189
  15.6 12.9 %collective-permute-start.3 = (f32[96,512]{1,0:T(8,128)S(1)}, f32[96,512]{1,0:T(8,128)S(1)}, u32[]{:S(2)}, u32[]{:S(2)}) collective-permute-start(f32[96,512]{1,0:T(8,128)S(1)} %get-tuple-element.26), channel_id=1, source_target_pairs={{0,2},{1,3},{2,0},{3,1},{4,6},{5,7},{6,4},{7,5},{8,10},{9,11},{10,... | collective-permute-start | bytes 589832 | tf_op jit(solution)/shard_map/ppermute | solution.py:189
  16.5 11.9 %copy-start.2 = (s32[1536,1]{1,0:T(8,128)}, s32[1536,1]{1,0:T(8,128)S(1)}, u32[]{:S(2)}) copy-start(s32[1536,1]{1,0:T(8,128)S(1)} %reshape.57.src_col.refs_3_) | copy-start | bytes 18436
  24.0 5.9 %copy-start.6 = (f32[384,512]{1,0:T(8,128)S(1)}, f32[384,512]{1,0:T(8,128)}, u32[]{:S(2)}) copy-start(f32[384,512]{1,0:T(8,128)} %refs_9_.1) | copy-start | bytes 2359300
  24.0 5.9 %collective-permute-start.4 = (f32[96,512]{1,0:T(8,128)S(1)}, f32[96,512]{1,0:T(8,128)S(1)}, u32[]{:S(2)}, u32[]{:S(2)}) collective-permute-start(f32[96,512]{1,0:T(8,128)S(1)} %get-tuple-element.25), channel_id=1, source_target_pairs={{0,8},{1,9},{2,10},{3,11},{4,12},{5,13},{6,14},{7,15},{8,0},{9,1},... | collective-permute-start | bytes 589832 | tf_op jit(solution)/shard_map/ppermute | solution.py:189
  40.4 0.9 copy-start.4
  41.3 0.9 copy-start.9
  42.2 0.7 copy-start.11
  42.9 1.1 copy-start.3
  44.0 1.1 copy-start.10
  45.2 11.3 %copy-start.5 = (f32[384,512]{1,0:T(8,128)S(1)}, f32[384,512]{1,0:T(8,128)}, u32[]{:S(2)}) copy-start(f32[384,512]{1,0:T(8,128)} %copy-done.4) | copy-start | bytes 2359300
  52.9 51.8 %copy-start = (f32[512,512]{1,0:T(8,128)S(1)}, f32[512,512]{1,0:T(8,128)}, u32[]{:S(2)}) copy-start(f32[512,512]{1,0:T(8,128)} %w_rev.1) | copy-start | bytes 3145732
  53.6 8.2 %collective-permute-start.6 = (f32[96,512]{1,0:T(8,128)S(1)}, f32[96,512]{1,0:T(8,128)S(1)}, u32[]{:S(2)}, u32[]{:S(2)}) collective-permute-start(f32[96,512]{1,0:T(8,128)S(1)} %get-tuple-element.20), channel_id=1, source_target_pairs={{0,31},{1,0},{2,1},{3,2},{4,3},{5,4},{6,5},{7,6},{8,7},{9,8},{10,9... | collective-permute-start | bytes 589832 | tf_op jit(solution)/shard_map/ppermute | solution.py:179
  56.5 48.1 %collective-permute-start.7 = (f32[96,512]{1,0:T(8,128)}, f32[96,512]{1,0:T(8,128)}, u32[]{:S(2)}, u32[]{:S(2)}) collective-permute-start(f32[96,512]{1,0:T(8,128)} %get-tuple-element.19), channel_id=1, source_target_pairs={{0,1},{1,2},{2,3},{3,4},{4,5},{5,6},{6,7},{7,8},{8,9},{9,10},{10,1... | collective-permute-start | bytes 589832 | tf_op jit(solution)/shard_map/ppermute | solution.py:179
  57.4 47.2 %collective-permute-start.10 = (f32[96,512]{1,0:T(8,128)}, f32[96,512]{1,0:T(8,128)}, u32[]{:S(2)}, u32[]{:S(2)}) collective-permute-start(f32[96,512]{1,0:T(8,128)} %get-tuple-element.22), channel_id=1, source_target_pairs={{0,8},{1,9},{2,10},{3,11},{4,12},{5,13},{6,14},{7,15},{8,0},{9,1},... | collective-permute-start | bytes 589832 | tf_op jit(solution)/shard_map/ppermute | solution.py:189
  57.4 47.2 %collective-permute-start.11 = (f32[96,512]{1,0:T(8,128)}, f32[96,512]{1,0:T(8,128)}, u32[]{:S(2)}, u32[]{:S(2)}) collective-permute-start(f32[96,512]{1,0:T(8,128)} %get-tuple-element.21), channel_id=1, source_target_pairs={{0,16},{1,17},{2,18},{3,19},{4,20},{5,21},{6,22},{7,23},{8,24},{9,... | collective-permute-start | bytes 589832 | tf_op jit(solution)/shard_map/ppermute | solution.py:189
  58.9 45.8 %collective-permute-start.8 = (f32[96,512]{1,0:T(8,128)}, f32[96,512]{1,0:T(8,128)}, u32[]{:S(2)}, u32[]{:S(2)}) collective-permute-start(f32[96,512]{1,0:T(8,128)} %get-tuple-element.24), channel_id=1, source_target_pairs={{0,1},{1,0},{2,3},{3,2},{4,5},{5,4},{6,7},{7,6},{8,9},{9,8},{10,11... | collective-permute-start | bytes 589832 | tf_op jit(solution)/shard_map/ppermute | solution.py:189
  61.8 42.9 %collective-permute-start.9 = (f32[96,512]{1,0:T(8,128)}, f32[96,512]{1,0:T(8,128)}, u32[]{:S(2)}, u32[]{:S(2)}) collective-permute-start(f32[96,512]{1,0:T(8,128)} %get-tuple-element.23), channel_id=1, source_target_pairs={{0,2},{1,3},{2,0},{3,1},{4,6},{5,7},{6,4},{7,5},{8,10},{9,11},{10,... | collective-permute-start | bytes 589832 | tf_op jit(solution)/shard_map/ppermute | solution.py:189
Sparse Core Ops, SparseCore 0:
  42.4 139.3 reduce-scatter.1

commit v2 on v1

--- a/solution.py
+++ b/solution.py
@@ -64,6 +64,15 @@
     gathered = gather_window(low, messages, high, src_col)
     terms = gathered * triplet_weight(basis[...], w_basis[...])
     agg[...] = pick(onehot_columns(tgt_row[...], messages.shape[0]), terms)
+
+
+def spread(target, index, value):
+    devices, rows, half = target.shape[2:]
+    for r, order in enumerate(routes(devices)):
+        for shard in range(devices):
+            target[index, r, place(shard, order)] = value[
+                shard * rows : (shard + 1) * rows, r * half : (r + 1) * half
+            ]
 
 
 def mlp_kernel(
@@ -108,13 +117,13 @@
     grad = cotangent[...]
     for layer in range(depth - 1, -1, -1):
         grad_pre = split(grad * slopes[layer])
-        weight_grads[layer] = dot3(states[layer], grad_pre, ((0,), (0,))) * scale
+        spread(weight_grads, layer, dot3(states[layer], grad_pre, ((0,), (0,))) * scale)
         grad = grad + dot3(grad_pre, weights[layer], ((1,), (1,)))
     grad0[...] = grad
     grad_msg[...] = grad * (1.0 + gate)
     g_rev = grad * msg * rev_slope
     grad_rev_proj[...] = g_rev
-    weight_grads[depth] = dot3(rev, split(g_rev), ((0,), (0,))) * scale
+    spread(weight_grads, depth, dot3(rev, split(g_rev), ((0,), (0,))) * scale)
 
 
 def back_kernel(
@@ -159,6 +168,163 @@
     out[edges - group :, :] = out[edges - group :, :] + from_next[...]
 
 
+def routes(devices):
+    levels = devices.bit_length() - 1
+    first = list(range(levels))
+    second = list(first)
+    if levels > 2:
+        second[1], second[2] = second[2], second[1]
+    return first, second
+
+
+def place(shard, order):
+    spot = 0
+    for bit in order:
+        spot = 2 * spot + ((shard >> bit) & 1)
+    return spot
+
+
+def greet(me, levels):
+    barrier = pltpu.get_barrier_semaphore()
+    for bit in range(levels):
+        pl.semaphore_signal(
+            barrier, inc=1, device_id=(me ^ (1 << bit),), device_id_type=pl.DeviceIdType.MESH
+        )
+    pl.semaphore_wait(barrier, levels)
+
+
+def send(source, target, send_sem, recv_sem, device):
+    copy = pltpu.make_async_remote_copy(
+        src_ref=source,
+        dst_ref=target,
+        send_sem=send_sem,
+        recv_sem=recv_sem,
+        device_id=(device,),
+        device_id_type=pl.DeviceIdType.MESH,
+    )
+    copy.start()
+    return copy
+
+
+class Halving:
+    def __init__(self, me, order, stages, inbox, send_sems, recv_sems):
+        self.me, self.order = me, order
+        self.stages, self.inbox = stages, inbox
+        self.sems = (send_sems, recv_sems)
+        self.copies = []
+
+    def start(self, step):
+        bit = self.order[step]
+        count = self.stages[step].shape[0] // 2
+        mine = (self.me // (1 << bit)) % 2
+        self.mine, self.count = mine, count
+        self.copies.append(
+            send(
+                self.stages[step].at[pl.ds((1 - mine) * count, count)],
+                self.inbox[step],
+                self.sems[0].at[step],
+                self.sems[1].at[step],
+                self.me ^ (1 << bit),
+            )
+        )
+
+    def finish(self, step):
+        self.copies[step].wait_recv()
+        kept = self.stages[step][pl.ds(self.mine * self.count, self.count)]
+        total = kept + self.inbox[step][...]
+        if step + 1 < len(self.order):
+            self.stages[step + 1][...] = total
+        return total
+
+
+def reduce_kernel(devices, parts, basis, layer_out, rev_out, basis_out, *scratch):
+    levels = devices.bit_length() - 1
+    matrices = parts.shape[0]
+    rows, half = parts.shape[3], parts.shape[4]
+    inboxes, scratch = scratch[:levels], scratch[levels:]
+    kept, scratch = scratch[: levels - 1], scratch[levels - 1 :]
+    basis_in, basis_sum, send_sems, recv_sems = scratch
+    me = lax.axis_index("edges")
+    greet(me, levels)
+    orders = routes(devices)
+    chains = []
+    for m in range(matrices):
+        for r in range(2):
+            c = 2 * m + r
+            stages = [parts.at[m, r]] + [ref.at[c] for ref in kept]
+            inbox = [ref.at[c] for ref in inboxes]
+            chains.append(
+                Halving(me, orders[r], stages, inbox, send_sems.at[c], recv_sems.at[c])
+            )
+    last = len(chains)
+    basis_sum[0] = basis[...]
+    copies = []
+    for step in range(levels):
+        copies.append(
+            send(
+                basis_sum.at[step],
+                basis_in.at[step],
+                send_sems.at[last, step],
+                recv_sems.at[last, step],
+                me ^ (1 << step),
+            )
+        )
+        for c, chain in enumerate(chains):
+            if step:
+                chain.finish(step - 1)
+            chain.start(step)
+        copies[step].wait_recv()
+        basis_sum[step + 1] = basis_sum[step] + basis_in[step]
+    for c, chain in enumerate(chains):
+        total = chain.finish(levels - 1)
+        m, r = c // 2, c % 2
+        for row in range(rows):
+            spot = slice(row * 2 * half + r * half, row * 2 * half + (r + 1) * half)
+            if m + 1 < matrices:
+                layer_out[m : m + 1, spot] = total[0, row : row + 1, :]
+            else:
+                rev_out[0:1, spot] = total[0, row : row + 1, :]
+    basis_out[...] = basis_sum[levels]
+    for chain in chains:
+        for copy in chain.copies:
+            copy.wait_send()
+    for copy in copies:
+        copy.wait_send()
+
+
+def reduce_parts(parts, basis):
+    devices = lax.axis_size("edges")
+    levels = devices.bit_length() - 1
+    matrices, lanes, _, rows, half = parts.shape
+    chains = matrices * lanes
+    flat = devices * rows * 2 * half // devices
+    specs = [pl.BlockSpec(memory_space=pltpu.VMEM)]
+    sizes = [devices >> (step + 1) for step in range(levels)]
+    scratch = [pltpu.VMEM((chains, size, rows, half), F32) for size in sizes]
+    scratch += [pltpu.VMEM((chains, size, rows, half), F32) for size in sizes[:-1]]
+    scratch += [
+        pltpu.VMEM((levels,) + basis.shape, F32),
+        pltpu.VMEM((levels + 1,) + basis.shape, F32),
+        pltpu.SemaphoreType.DMA((chains + 1, levels)),
+        pltpu.SemaphoreType.DMA((chains + 1, levels)),
+    ]
+    return pl.pallas_call(
+        lambda *refs: reduce_kernel(devices, *refs),
+        out_shape=[
+            jax.ShapeDtypeStruct((matrices - 1, flat), F32),
+            jax.ShapeDtypeStruct((1, flat), F32),
+            jax.ShapeDtypeStruct(basis.shape, F32),
+        ],
+        in_specs=specs * 2,
+        out_specs=specs * 3,
+        scratch_shapes=scratch,
+        compiler_params=pltpu.CompilerParams(
+            vmem_limit_bytes=VMEM_LIMIT, collective_id=0, has_side_effects=True
+        ),
+        name="reduce",
+    )(parts, basis)
+
+
 def call(kernel, name, shapes, flops, *args):
     specs = [pl.BlockSpec(memory_space=pltpu.VMEM)]
     return pl.pallas_call(
@@ -208,7 +374,8 @@
     depth = w_layers.shape[0]
     tiles = tile_block.shape[0]
     slots = tri_source.shape[0]
-    scale = float(edges * lax.axis_size("edges")) ** (-0.5)
+    devices = lax.axis_size("edges")
+    scale = float(edges * devices) ** (-0.5)
     low = shift(messages[edges - halo :], 1)
     high = shift(messages[:halo], -1)
     arrived = exchange(messages)
@@ -236,7 +403,8 @@
     out, grad0, grad_msg, g_rev, weight_grads = call(
         lambda *refs: mlp_kernel(scale, *refs),
         "mlp",
-        [(edges, width)] * 4 + [(depth + 1, width, width)],
+        [(edges, width)] * 4
+        + [(depth + 1, 2, devices, width // devices, width // 2)],
         6 * 9 * edges * width * width,
         messages,
         agg,
@@ -246,8 +414,6 @@
         w_layers,
         cotangent,
     )
-    shares = lax.psum_scatter(weight_grads, "edges", scatter_dimension=1, tiled=True)
-    shares = shares.reshape(depth + 1, -1)
     back = exchange(g_rev)
     window_grad, basis_grad = call(
         lambda *refs: back_kernel(scale, *refs),
@@ -266,7 +432,7 @@
     )
     from_next = shift(window_grad[:halo], -1)
     from_prev = shift(window_grad[halo + edges :], 1)
-    grad_basis = lax.psum(basis_grad, "edges")
+    layer_share, rev_share, grad_basis = reduce_parts(weight_grads, basis_grad)
     (grad_out,) = call(
         end_kernel,
         "end",
@@ -280,7 +446,7 @@
         slot_col,
         w_rev,
     )
-    return (out, grad_out, shares[:depth], shares[depth], grad_basis)
+    return (out, grad_out, layer_share, rev_share.reshape(-1), grad_basis)
 
 
 def solution(mesh):

time: 192 us -> 84.4 us (0.44)
  waiting for transfers between devices: 84.7 us -> 11.3 us
  blocking collectives: 42.9 us -> 0 us
  Pallas kernels: 25.9 us -> 54.6 us
  between operations: 14.9 us -> 1.53 us
  local copies, waits for them, and re-layouts: 11.7 us -> 3.93 us
    reduce_scatter x1 -> x0, waiting for transfers between devices: 73.8 us -> none  [on_device(): lax.psum_scatter(weight_grads, 'edges', scatter_dimension=1, tiled=True)]
    psum x1 -> x0, blocking collectives: 42.9 us -> none  [on_device(): grad_basis = lax.psum(basis_grad, 'edges')]
    pallas_call x0 -> x1, Pallas kernels: none -> 30 us  [reduce_parts(): pl.pallas_call(lambda *refs: reduce_kernel(devices, *refs), out_shape=[ja...]
    unnamed x34 -> x19, local copies, waits for them, and re-layouts: 7.4 us -> 1.89 us
  transfers between devices with their start and end apart: 13 -> 12, of which waited for: 4 -> 3; matrix products, arithmetic and copies ran while one was open for 2% -> 3% of each run, Pallas kernels for 8% -> 41%
where the time goes in v2:
time: 84.4 us; the launch traced here: 84.2 us
  Pallas kernels  54.6 us (65%)
  starting transfers between devices  11.4 us (14%)
  waiting for transfers between devices  11.3 us (13%)
  local copies, waits for them, and re-layouts  3.93 us (5%)
  between operations  1.53 us (2%)
  other arithmetic  1.43 us (2%)
    pallas_call x1, Pallas kernels, reduce_parts(): pl.pallas_call(lambda *refs: reduce_kernel(devices, *refs), out_shape=[ja...  30 us
    pallas_call x4, Pallas kernels, call(): pl.pallas_call(kernel, out_shape=[jax.ShapeDtypeStruct(shape, F32) for sh...  24.6 us
    ppermute x4, starting transfers between devices, shift(): lax.ppermute(block, 'edges', [(i, (i + distance) % count) for i in range(...  10.2 us
    ppermute x4, waiting for transfers between devices, shift(): lax.ppermute(block, 'edges', [(i, (i + distance) % count) for i in range(...  9.73 us
    unnamed x19, local copies, waits for them, and re-layouts  1.89 us
  transfers between devices with their start and end apart: 12, of which 3 were waited for; matrix products, arithmetic and copies ran while one was open for 3% of the time, Pallas kernels for 41%

profile of v2, /device:TPU:0, one launch (start us, length us, event | category | flops | bytes accessed | tf_op | source)
XLA Modules:
  0.0 84.2 jit_solution(9362609162860909725)
XLA Ops:
  0.7 1.3 %fusion.3 = (f32[96,512]{1,0:T(8,128)S(1)}, f32[96,512]{1,0:T(8,128)S(1)}, f32[96,512]{1,0:T(8,128)S(1)}, f32[96,512]{1,0:T(8,128)S(1)}) fusion(f32[384,512]{1,0:T(8,128)} %refs_1_.1), kind=kLoop, calls=%fused_computation.6 | loop fusion | bytes 1572864 | tf_op jit(solution)/shard_map/slice | solution.py:355
  2.0 6.4 %collective-permute-start.1 = (f32[96,512]{1,0:T(8,128)S(1)}, f32[96,512]{1,0:T(8,128)S(1)}, u32[]{:S(2)}, u32[]{:S(2)}) collective-permute-start(f32[96,512]{1,0:T(8,128)S(1)} %get-tuple-element.33), channel_id=1, source_target_pairs={{0,31},{1,0},{2,1},{3,2},{4,3},{5,4},{6,5},{7,6},{8,7},{9,8},{10,9... | collective-permute-start | bytes 589832 | tf_op jit(solution)/shard_map/ppermute | solution.py:345
  8.4 0.5 collective-permute-start
  9.0 0.0 collective-permute-start.5
  9.0 0.0 collective-permute-start.3
  9.6 0.7 broadcast_multiply_fusion
  10.3 0.8 fusion
  11.1 0.3 select_n.15.refs_5_
  11.3 0.3 reshape.57.src_col.refs_3_
  11.6 0.1 reshape.58.refs_6_.slot_col
  11.7 5.6 %collective-permute-done.low.refs_0_ = f32[96,512]{1,0:T(8,128)S(1)} collective-permute-done((f32[96,512]{1,0:T(8,128)S(1)}, f32[96,512]{1,0:T(8,128)S(1)}, u32[]{:S(2)}, u32[]{:S(2)}) %collective-permute-start) | collective-permute-done | bytes 196640 | tf_op jit(solution)/shard_map/ppermute | solution.py:345
  17.4 0.0 collective-permute-start.4
  17.4 0.0 collective-permute-done.1.high.refs_2_
  17.4 4.4 %agg.1.refs_1_ = f32[384,512]{1,0:T(8,128)S(1)} custom-call(f32[96,512]{1,0:T(8,128)S(1)} %collective-permute-done.low.refs_0_, f32[384,512]{1,0:T(8,128)S(1)} %copy-done.2, f32[96,512]{1,0:T(8,128)S(1)} %collective-permute-done.1.high.refs_2_, s32[1536,1]{1,0:T(8,128)S(1)} %reshape.57.src_col.refs_3_, s32[1,1536]{1,0:T(1,128)S(1)} %select_n.13.tgt_row, ...), custom_call_target="tpu_custom_call" | custom-call | flops 3019898880 | bytes 4194304 | tf_op jit(solution)/shard_map/agg/pallas_call | solution.py:330
  21.8 0.0 collective-permute-done.2.refs_2_
  21.8 0.0 collective-permute-done.5.refs_5_
  21.9 1.6 %collective-permute-done.4.refs_4_ = f32[96,512]{1,0:T(8,128)S(1)} collective-permute-done((f32[96,512]{1,0:T(8,128)S(1)}, f32[96,512]{1,0:T(8,128)S(1)}, u32[]{:S(2)}, u32[]{:S(2)}) %collective-permute-start.4) | collective-permute-done | bytes 196640 | tf_op jit(solution)/shard_map/ppermute | solution.py:355
  23.4 10.5 %mlp.1 = (f32[384,512]{1,0:T(8,128)}, f32[384,512]{1,0:T(8,128)S(1)}, f32[384,512]{1,0:T(8,128)S(1)}, f32[384,512]{1,0:T(8,128)S(1)}, f32[3,2,32,16,256]{4,3,2,1,0:T(8,128)}) custom-call(f32[384,512]{1,0:T(8,128)S(1)} %copy-done.2, f32[384,512]{1,0:T(8,128)S(1)} %agg.1.refs_1_, f32[96,512]{1,0:T(8,128)S(1)} %collective-permute-done.2.refs_2_, ...), custom_call_target="tpu_custom_call" | custom-call | flops 5435817984 | bytes 4194304 | tf_op jit(solution)/shard_map/mlp/pallas_call | solution.py:330
  34.0 7.6 %back.1 = (f32[576,512]{1,0:T(8,128)S(1)}, f32[16,512]{1,0:T(8,128)S(1)}) custom-call(f32[96,512]{1,0:T(8,128)S(1)} %collective-permute-done.low.refs_0_, f32[384,512]{1,0:T(8,128)S(1)} %copy-done.2, f32[96,512]{1,0:T(8,128)S(1)} %collective-permute-done.1.high.refs_2_, s32[1536,1]{1,0:T(8,128)S(1)} %reshape.57.src_col.refs_3_, ...), custom_call_target="tpu_custom_call" | custom-call | flops 4831838208 | bytes 4194304 | tf_op jit(solution)/shard_map/back/pallas_call | solution.py:330
  41.7 3.3 %collective-permute-start.6 = (f32[96,512]{1,0:T(8,128)S(1)}, f32[96,512]{1,0:T(8,128)S(1)}, u32[]{:S(2)}, u32[]{:S(2)}) collective-permute-start(f32[96,512]{1,0:T(8,128)S(1)} %get-tuple-element.26), channel_id=1, source_target_pairs={{0,31},{1,0},{2,1},{3,2},{4,3},{5,4},{6,5},{7,6},{8,7},{9,8},{10,9... | collective-permute-start | bytes 589832 | tf_op jit(solution)/shard_map/ppermute | solution.py:345
  45.0 0.1 fusion.2
  45.0 0.1 collective-permute-start.10
  45.1 1.0 %collective-permute-start.11 = (f32[96,512]{1,0:T(8,128)S(1)}, f32[96,512]{1,0:T(8,128)S(1)}, u32[]{:S(2)}, u32[]{:S(2)}) collective-permute-start(f32[96,512]{1,0:T(8,128)S(1)} %get-tuple-element.27), channel_id=1, source_target_pairs={{0,16},{1,17},{2,18},{3,19},{4,20},{5,21},{6,22},{7,23},{8,24},{9,... | collective-permute-start | bytes 589832 | tf_op jit(solution)/shard_map/ppermute | solution.py:355
  46.1 0.0 collective-permute-start.8
  46.1 4.1 %collective-permute-done.6.from_next = f32[96,512]{1,0:T(8,128)S(1)} collective-permute-done((f32[96,512]{1,0:T(8,128)S(1)}, f32[96,512]{1,0:T(8,128)S(1)}, u32[]{:S(2)}, u32[]{:S(2)}) %collective-permute-start.6) | collective-permute-done | bytes 196640 | tf_op jit(solution)/shard_map/ppermute | solution.py:345
  50.2 30.0 %reduce.1 = (f32[2,8192]{1,0:T(2,128)S(1)}, f32[1,8192]{1,0:T(1,128)S(1)}, f32[16,512]{1,0:T(8,128)S(1)}) custom-call(f32[3,2,32,16,256]{4,3,2,1,0:T(8,128)S(1)} %copy-done, f32[16,512]{1,0:T(8,128)S(1)} %get-tuple-element.21.refs_1_), custom_call_target="tpu_custom_call" | custom-call | tf_op jit(solution)/shard_map/reduce/pallas_call | solution.py:311
  80.3 0.0 collective-permute-done.10.b2
  80.3 0.0 collective-permute-done.11.b3
  80.4 2.0 %end.1 = f32[384,512]{1,0:T(8,128)} custom-call(f32[384,512]{1,0:T(8,128)S(1)} %get-tuple-element.16.grad_msg, f32[576,512]{1,0:T(8,128)S(1)} %get-tuple-element.18.window_grad, f32[96,512]{1,0:T(8,128)S(1)} %collective-permute-done.6.from_next, f32[96,512]{1,0:T(8,128)S(1)} %collective-permute-done.7.from_prev, f32[96,512]{1,0:T(8,128)S(1)} %collective-permute-done.8.b0, ...), custom_call_target="tpu_custom_call" | custom-call | flops 603979776 | bytes 4194304 | tf_op jit(solution)/shard_map/end/pallas_call | solution.py:330
  82.3 0.6 copy.25
  83.0 0.6 copy.26
  83.6 0.6 copy.27
  (27 shorter events, 0.1 us)
Async XLA Ops:
  0.6 16.8 %copy-start.2 = (f32[384,512]{1,0:T(8,128)S(1)}, f32[384,512]{1,0:T(8,128)}, u32[]{:S(2)}) copy-start(f32[384,512]{1,0:T(8,128)} %refs_1_.1) | copy-start | bytes 2359300
  0.6 10.7 %copy-start.6 = (s32[1536]{0:T(1024)S(1)}, s32[1536]{0:T(1024)}, u32[]{:S(2)}) copy-start(s32[1536]{0:T(1024)} %param.14) | copy-start | bytes 18436
  0.7 11.0 %copy-start.7 = (s32[384]{0:T(512)S(1)}, s32[384]{0:T(512)}, u32[]{:S(2)}) copy-start(s32[384]{0:T(512)} %param.12) | copy-start | bytes 4612
  0.7 16.7 %copy-start.4 = (f32[16,1536]{1,0:T(8,128)S(1)}, f32[16,1536]{1,0:T(8,128)}, u32[]{:S(2)}) copy-start(f32[16,1536]{1,0:T(8,128)} %refs_6_.1) | copy-start | bytes 294916
  0.7 16.7 %copy-start.5 = (f32[16,512]{1,0:T(8,128)S(1)}, f32[16,512]{1,0:T(8,128)}, u32[]{:S(2)}) copy-start(f32[16,512]{1,0:T(8,128)} %refs_7_.3) | copy-start | bytes 98308
  2.0 15.4 %collective-permute-start.1 = (f32[96,512]{1,0:T(8,128)S(1)}, f32[96,512]{1,0:T(8,128)S(1)}, u32[]{:S(2)}, u32[]{:S(2)}) collective-permute-start(f32[96,512]{1,0:T(8,128)S(1)} %get-tuple-element.33), channel_id=1, source_target_pairs={{0,31},{1,0},{2,1},{3,2},{4,3},{5,4},{6,5},{7,6},{8,7},{9,8},{10,9... | collective-permute-start | bytes 589832 | tf_op jit(solution)/shard_map/ppermute | solution.py:345
  8.4 13.4 %collective-permute-start.2 = (f32[96,512]{1,0:T(8,128)S(1)}, f32[96,512]{1,0:T(8,128)S(1)}, u32[]{:S(2)}, u32[]{:S(2)}) collective-permute-start(f32[96,512]{1,0:T(8,128)S(1)} %get-tuple-element.33), channel_id=1, source_target_pairs={{0,1},{1,0},{2,3},{3,2},{4,5},{5,4},{6,7},{7,6},{8,9},{9,8},{10,11... | collective-permute-start | bytes 589832 | tf_op jit(solution)/shard_map/ppermute | solution.py:355
  8.4 8.9 %collective-permute-start = (f32[96,512]{1,0:T(8,128)S(1)}, f32[96,512]{1,0:T(8,128)S(1)}, u32[]{:S(2)}, u32[]{:S(2)}) collective-permute-start(f32[96,512]{1,0:T(8,128)S(1)} %get-tuple-element.34), channel_id=1, source_target_pairs={{0,1},{1,2},{2,3},{3,4},{4,5},{5,6},{6,7},{7,8},{8,9},{9,10},{10,1... | collective-permute-start | bytes 589832 | tf_op jit(solution)/shard_map/ppermute | solution.py:345
  9.0 12.9 %collective-permute-start.5 = (f32[96,512]{1,0:T(8,128)S(1)}, f32[96,512]{1,0:T(8,128)S(1)}, u32[]{:S(2)}, u32[]{:S(2)}) collective-permute-start(f32[96,512]{1,0:T(8,128)S(1)} %get-tuple-element.34), channel_id=1, source_target_pairs={{0,16},{1,17},{2,18},{3,19},{4,20},{5,21},{6,22},{7,23},{8,24},{9,... | collective-permute-start | bytes 589832 | tf_op jit(solution)/shard_map/ppermute | solution.py:355
  9.0 12.9 %collective-permute-start.3 = (f32[96,512]{1,0:T(8,128)S(1)}, f32[96,512]{1,0:T(8,128)S(1)}, u32[]{:S(2)}, u32[]{:S(2)}) collective-permute-start(f32[96,512]{1,0:T(8,128)S(1)} %get-tuple-element.32), channel_id=1, source_target_pairs={{0,2},{1,3},{2,0},{3,1},{4,6},{5,7},{6,4},{7,5},{8,10},{9,11},{10,... | collective-permute-start | bytes 589832 | tf_op jit(solution)/shard_map/ppermute | solution.py:355
  17.4 6.1 %copy-start.3 = (f32[384,512]{1,0:T(8,128)S(1)}, f32[384,512]{1,0:T(8,128)}, u32[]{:S(2)}) copy-start(f32[384,512]{1,0:T(8,128)} %refs_9_.1) | copy-start | bytes 2359300
  17.4 6.1 %collective-permute-start.4 = (f32[96,512]{1,0:T(8,128)S(1)}, f32[96,512]{1,0:T(8,128)S(1)}, u32[]{:S(2)}, u32[]{:S(2)}) collective-permute-start(f32[96,512]{1,0:T(8,128)S(1)} %get-tuple-element.31), channel_id=1, source_target_pairs={{0,8},{1,9},{2,10},{3,11},{4,12},{5,13},{6,14},{7,15},{8,0},{9,1},... | collective-permute-start | bytes 589832 | tf_op jit(solution)/shard_map/ppermute | solution.py:355
  34.0 16.2 %copy-start = (f32[3,2,32,16,256]{4,3,2,1,0:T(8,128)S(1)}, f32[3,2,32,16,256]{4,3,2,1,0:T(8,128)}, u32[]{:S(2)}) copy-start(f32[3,2,32,16,256]{4,3,2,1,0:T(8,128)} %get-tuple-element.20.refs_0_) | copy-start | bytes 9437188
  41.7 8.6 %collective-permute-start.6 = (f32[96,512]{1,0:T(8,128)S(1)}, f32[96,512]{1,0:T(8,128)S(1)}, u32[]{:S(2)}, u32[]{:S(2)}) collective-permute-start(f32[96,512]{1,0:T(8,128)S(1)} %get-tuple-element.26), channel_id=1, source_target_pairs={{0,31},{1,0},{2,1},{3,2},{4,3},{5,4},{6,5},{7,6},{8,7},{9,8},{10,9... | collective-permute-start | bytes 589832 | tf_op jit(solution)/shard_map/ppermute | solution.py:345
  45.0 35.3 %collective-permute-start.7 = (f32[96,512]{1,0:T(8,128)S(1)}, f32[96,512]{1,0:T(8,128)S(1)}, u32[]{:S(2)}, u32[]{:S(2)}) collective-permute-start(f32[96,512]{1,0:T(8,128)S(1)} %get-tuple-element.25), channel_id=1, source_target_pairs={{0,1},{1,2},{2,3},{3,4},{4,5},{5,6},{6,7},{7,8},{8,9},{9,10},{10,1... | collective-permute-start | bytes 589832 | tf_op jit(solution)/shard_map/ppermute | solution.py:345
  45.0 35.4 %copy-start.1 = (f32[512,512]{1,0:T(8,128)S(1)}, f32[512,512]{1,0:T(8,128)}, u32[]{:S(2)}) copy-start(f32[512,512]{1,0:T(8,128)} %w_rev.1) | copy-start | bytes 3145732
  45.0 35.3 %collective-permute-start.10 = (f32[96,512]{1,0:T(8,128)S(1)}, f32[96,512]{1,0:T(8,128)S(1)}, u32[]{:S(2)}, u32[]{:S(2)}) collective-permute-start(f32[96,512]{1,0:T(8,128)S(1)} %get-tuple-element.28), channel_id=1, source_target_pairs={{0,8},{1,9},{2,10},{3,11},{4,12},{5,13},{6,14},{7,15},{8,0},{9,1},... | collective-permute-start | bytes 589832 | tf_op jit(solution)/shard_map/ppermute | solution.py:355
  45.1 35.2 %collective-permute-start.11 = (f32[96,512]{1,0:T(8,128)S(1)}, f32[96,512]{1,0:T(8,128)S(1)}, u32[]{:S(2)}, u32[]{:S(2)}) collective-permute-start(f32[96,512]{1,0:T(8,128)S(1)} %get-tuple-element.27), channel_id=1, source_target_pairs={{0,16},{1,17},{2,18},{3,19},{4,20},{5,21},{6,22},{7,23},{8,24},{9,... | collective-permute-start | bytes 589832 | tf_op jit(solution)/shard_map/ppermute | solution.py:355
  46.1 34.2 %collective-permute-start.8 = (f32[96,512]{1,0:T(8,128)S(1)}, f32[96,512]{1,0:T(8,128)S(1)}, u32[]{:S(2)}, u32[]{:S(2)}) collective-permute-start(f32[96,512]{1,0:T(8,128)S(1)} %get-tuple-element.30), channel_id=1, source_target_pairs={{0,1},{1,0},{2,3},{3,2},{4,5},{5,4},{6,7},{7,6},{8,9},{9,8},{10,11... | collective-permute-start | bytes 589832 | tf_op jit(solution)/shard_map/ppermute | solution.py:355
  50.2 30.1 %collective-permute-start.9 = (f32[96,512]{1,0:T(8,128)S(1)}, f32[96,512]{1,0:T(8,128)S(1)}, u32[]{:S(2)}, u32[]{:S(2)}) collective-permute-start(f32[96,512]{1,0:T(8,128)S(1)} %get-tuple-element.29), channel_id=1, source_target_pairs={{0,2},{1,3},{2,0},{3,1},{4,6},{5,7},{6,4},{7,5},{8,10},{9,11},{10,... | collective-permute-start | bytes 589832 | tf_op jit(solution)/shard_map/ppermute | solution.py:355

commit v3 on v1

v3 whole, which is shorter than its diff:
```python
import jax
import jax.numpy as jnp
from jax import lax
from jax.experimental import pallas as pl
from jax.experimental.pallas import tpu as pltpu
from jax.sharding import PartitionSpec as P

F32 = jnp.float32
BF16 = jnp.bfloat16
VMEM_LIMIT = 56 * 1024 * 1024


def split(value):
    high = value.astype(BF16)
    low = (value - high.astype(F32)).astype(BF16)
    return high, low


def dot(left, right, dims=((1,), (0,))):
    return lax.dot_general(left, right, (dims, ((), ())), preferred_element_type=F32)


def dot3(left, right, dims=((1,), (0,))):
    (lh, ll), (rh, rl) = left, right
    return dot(lh, rh, dims) + dot(lh, rl, dims) + dot(ll, rh, dims)


def pick(onehot, value):
    high, low = split(value)
    return dot(onehot, high) + dot(onehot, low)


def onehot_rows(column, width):
    ids = lax.broadcasted_iota(jnp.int32, (column.shape[0], width), 1)
    return jnp.where(column == ids, 1.0, 0.0).astype(BF16)


def onehot_columns(row, height):
    ids = lax.broadcasted_iota(jnp.int32, (height, row.shape[1]), 0)
    return jnp.where(row == ids, 1.0, 0.0).astype(BF16)


def silu_pair(values):
    sigma = jax.nn.sigmoid(values)
    return values * sigma, sigma * (1.0 + values * (1.0 - sigma))


def triplet_weight(basis, w_basis):
    bh, bl = split(basis)
    wh, wl = split(w_basis)
    return dot(
        jnp.concatenate([bh, bl, bh], axis=0),
        jnp.concatenate([wh, wh, wl], axis=0),
        ((0,), (0,)),
    )


def spread(target, index, value):
    devices, rows, half = target.shape[2:]
    for r, order in enumerate(routes(devices)):
        for shard in range(devices):
            target[index, r, place(shard, order)] = value[
                shard * rows : (shard + 1) * rows, r * half : (r + 1) * half
            ]


def routes(devices):
    levels = devices.bit_length() - 1
    first = list(range(levels))
    second = list(first)
    if levels > 2:
        second[1], second[2] = second[2], second[1]
    return first, second


def place(shard, order):
    spot = 0
    for bit in order:
        spot = 2 * spot + ((shard >> bit) & 1)
    return spot


def send(source, target, send_sem, recv_sem, device):
    copy = pltpu.make_async_remote_copy(
        src_ref=source,
        dst_ref=target,
        send_sem=send_sem,
        recv_sem=recv_sem,
        device_id=(device,),
        device_id_type=pl.DeviceIdType.MESH,
    )
    copy.start()
    return copy


def greet(me, devices):
    levels = devices.bit_length() - 1
    barrier = pltpu.get_barrier_semaphore()
    others = [me ^ (1 << bit) for bit in range(levels)]
    others += [lax.rem(me + 1, devices), lax.rem(me + devices - 1, devices)]
    for other in others:
        pl.semaphore_signal(
            barrier, inc=1, device_id=(other,), device_id_type=pl.DeviceIdType.MESH
        )
    pl.semaphore_wait(barrier, len(others))


class Halving:
    def __init__(self, me, order, stages, inbox, send_sems, recv_sems):
        self.me, self.order = me, order
        self.stages, self.inbox = stages, inbox
        self.sems = (send_sems, recv_sems)
        self.copies = []

    def start(self, step):
        bit = self.order[step]
        count = self.stages[step].shape[0] // 2
        mine = (self.me // (1 << bit)) % 2
        self.mine, self.count = mine, count
        self.copies.append(
            send(
                self.stages[step].at[pl.ds((1 - mine) * count, count)],
                self.inbox[step],
                self.sems[0].at[step],
                self.sems[1].at[step],
                self.me ^ (1 << bit),
            )
        )

    def finish(self, step):
        self.copies[step].wait_recv()
        kept = self.stages[step][pl.ds(self.mine * self.count, self.count)]
        total = kept + self.inbox[step][...]
        if step + 1 < len(self.order):
            self.stages[step + 1][...] = total
        return total

    def advance(self):
        step = len(self.copies)
        if step < len(self.order):
            if step:
                self.finish(step - 1)
            self.start(step)


def block_kernel(
    devices,
    scale,
    messages,
    src_col,
    src_row,
    tgt_col,
    tgt_row,
    slot_col,
    basis,
    w_basis,
    w_rev,
    w_layers,
    cotangent,
    out,
    grad_out,
    layer_out,
    rev_out,
    basis_out,
    *scratch,
):
    levels = devices.bit_length() - 1
    edges, width = messages.shape
    halo = group = edges // 4
    depth = w_layers.shape[0]
    inboxes, scratch = scratch[:levels], scratch[levels:]
    kept, scratch = scratch[: levels - 1], scratch[levels - 1 :]
    (
        parts,
        window,
        arrived,
        returned,
        g_rev,
        gathered,
        tri_weight,
        window_grad,
        rims,
        basis_in,
        basis_sum,
        send_sems,
        recv_sems,
        row_send,
        row_recv,
    ) = scratch
    me = lax.axis_index("edges")
    ahead, behind = lax.rem(me + 1, devices), lax.rem(me + devices - 1, devices)
    bits = (0, levels // 3, 2 * levels // 3, levels - 1)
    greet(me, devices)

    def row_copy(source, target, slot, device):
        return send(source, target, row_send.at[slot], row_recv.at[slot], device)

    halos = [
        row_copy(messages.at[pl.ds(edges - halo, halo)], window.at[pl.ds(0, halo)], 0, ahead),
        row_copy(
            messages.at[pl.ds(0, halo)], window.at[pl.ds(halo + edges, halo)], 1, behind
        ),
    ]

    def exchange(rows, target, first):
        copies = [None] * 4
        for k in (3, 2, 1, 0):
            copies[k] = row_copy(
                rows.at[pl.ds(k * group, group)], target.at[k], first + k, me ^ (1 << bits[k])
            )
        return copies

    def collect(copies, target):
        highs, lows = [], []
        for k in range(4):
            onehot = onehot_rows(slot_col[k * group : (k + 1) * group, :], group)
            copies[k].wait_recv()
            ah, al = split(target[k])
            highs.append(dot(onehot, ah).astype(BF16))
            lows.append(dot(onehot, al).astype(BF16))
        return jnp.concatenate(highs, axis=0), jnp.concatenate(lows, axis=0)

    forth = exchange(messages, arrived, 2)
    window[halo : halo + edges, :] = messages[...]
    tri_weight[...] = triplet_weight(basis[...], w_basis[...])
    weights = [split(w_layers[layer]) for layer in range(depth)]
    weight_rev = split(w_rev[...])
    for copy in halos:
        copy.wait_recv()
    gathered[...] = pick(onehot_rows(src_col[...], edges + 2 * halo), window[...])
    agg = pick(onehot_columns(tgt_row[...], edges), gathered[...] * tri_weight[...])

    rev = collect(forth, arrived)
    gate, rev_slope = silu_pair(dot3(rev, weight_rev))
    msg = messages[...]
    hidden = msg + agg + msg * gate
    states, slopes, grad_pres = [], [], [None] * depth
    for layer in range(depth):
        state = split(hidden)
        act, slope = silu_pair(dot3(state, weights[layer]))
        hidden = hidden + act
        states.append(state)
        slopes.append(slope)
    out[...] = hidden
    grad = cotangent[...]
    for layer in range(depth - 1, -1, -1):
        grad_pres[layer] = split(grad * slopes[layer])
        grad = grad + dot3(grad_pres[layer], weights[layer], ((1,), (1,)))
    g_rev_rows = grad * msg * rev_slope
    g_rev[...] = g_rev_rows
    back = exchange(g_rev, returned, 6)
    grad_out[...] = grad * (1.0 + gate)

    orders = routes(devices)
    chains = []
    for m in range(depth + 1):
        for r in range(2):
            c = 2 * m + r
            stages = [parts.at[m, r]] + [ref.at[c] for ref in kept]
            inbox = [ref.at[c] for ref in inboxes]
            chains.append(
                Halving(me, orders[r], stages, inbox, send_sems.at[c], recv_sems.at[c])
            )

    def advance(m):
        chains[2 * m].advance()
        chains[2 * m + 1].advance()

    for layer in range(depth - 1, -1, -1):
        product = dot3(states[layer], grad_pres[layer], ((0,), (0,)))
        spread(parts, layer, product * scale)
        for m in range(depth - 1, layer - 1, -1):
            advance(m)
    spread(parts, depth, dot3(rev, split(g_rev_rows), ((0,), (0,))) * scale)
    advance(depth)
    advance(0)
    grad_prod = pick(onehot_rows(tgt_col[...], edges), grad)
    basis_sum[0] = dot3(split(basis[...]), split(grad_prod * gathered[...])) * scale
    last = len(chains)
    basis_copies = []

    def basis_advance():
        step = len(basis_copies)
        if step:
            basis_copies[-1].wait_recv()
            basis_sum[step] = basis_sum[step - 1] + basis_in[step - 1]
        if step < levels:
            basis_copies.append(
                send(
                    basis_sum.at[step],
                    basis_in.at[step],
                    send_sems.at[last, step],
                    recv_sems.at[last, step],
                    me ^ (1 << step),
                )
            )

    basis_advance()
    advance(depth)
    window_grad[...] = pick(
        onehot_columns(src_row[...], edges + 2 * halo), grad_prod * tri_weight[...]
    )
    rim_copies = [
        row_copy(window_grad.at[pl.ds(0, halo)], rims.at[0], 10, behind),
        row_copy(window_grad.at[pl.ds(halo + edges, halo)], rims.at[1], 11, ahead),
    ]
    for m in range(depth - 1, -1, -1):
        advance(m)
    basis_advance()
    grad_out[...] = (
        grad_out[...]
        + window_grad[halo : halo + edges, :]
        + dot3(collect(back, returned), weight_rev, ((1,), (1,)))
    )
    advance(depth)
    for step in range(2, levels):
        for m in list(range(depth - 1, -1, -1)) + [depth]:
            advance(m)
        basis_advance()
    rim_copies[0].wait_recv()
    grad_out[edges - halo :, :] = grad_out[edges - halo :, :] + rims[0]
    rim_copies[1].wait_recv()
    grad_out[:halo, :] = grad_out[:halo, :] + rims[1]
    rows, half = parts.shape[3], parts.shape[4]
    for c, chain in enumerate(chains):
        while len(chain.copies) < levels:
            chain.advance()
        total = chain.finish(levels - 1)
        m, r = c // 2, c % 2
        for row in range(rows):
            spot = slice(row * width + r * half, row * width + (r + 1) * half)
            if m < depth:
                layer_out[m : m + 1, spot] = total[0, row : row + 1, :]
            else:
                rev_out[0:1, spot] = total[0, row : row + 1, :]
    basis_advance()
    basis_out[...] = basis_sum[levels]
    for copy in halos + forth + back + rim_copies + basis_copies:
        copy.wait_send()
    for chain in chains:
        for copy in chain.copies:
            copy.wait_send()


def on_device(
    messages,
    rev_slot,
    tri_basis,
    tri_source,
    tri_target,
    tile_block,
    tile_count,
    w_basis,
    w_rev,
    w_layers,
    cotangent,
):
    devices = lax.axis_size("edges")
    levels = devices.bit_length() - 1
    edges, width = messages.shape
    halo = edges // 4
    depth = w_layers.shape[0]
    tiles = tile_block.shape[0]
    slots = tri_source.shape[0]
    scale = float(edges * devices) ** (-0.5)

    live = jnp.arange(tiles, dtype=jnp.int32) < tile_count[0]
    target = tile_block[:, None] * 128 + tri_target.reshape(tiles, 128)
    target = jnp.where(live[:, None], target, -1)
    tgt_row, tgt_col = target.reshape(1, slots), target.reshape(slots, 1)
    src_row, src_col = tri_source.reshape(1, slots), tri_source.reshape(slots, 1)
    slot_col = rev_slot.reshape(edges, 1)

    rows, half, chains = width // devices, width // 2, 2 * (depth + 1)
    sizes = [devices >> (step + 1) for step in range(levels)]
    scratch = [pltpu.VMEM((chains, size, rows, half), F32) for size in sizes]
    scratch += [pltpu.VMEM((chains, size, rows, half), F32) for size in sizes[:-1]]
    scratch += [
        pltpu.VMEM((depth + 1, 2, devices, rows, half), F32),
        pltpu.VMEM((edges + 2 * halo, width), F32),
        pltpu.VMEM((4, halo, width), F32),
        pltpu.VMEM((4, halo, width), F32),
        pltpu.VMEM((edges, width), F32),
        pltpu.VMEM((slots, width), F32),
        pltpu.VMEM((slots, width), F32),
        pltpu.VMEM((edges + 2 * halo, width), F32),
        pltpu.VMEM((2, halo, width), F32),
        pltpu.VMEM((levels,) + w_basis.shape, F32),
        pltpu.VMEM((levels + 1,) + w_basis.shape, F32),
        pltpu.SemaphoreType.DMA((chains + 1, levels)),
        pltpu.SemaphoreType.DMA((chains + 1, levels)),
        pltpu.SemaphoreType.DMA((12,)),
        pltpu.SemaphoreType.DMA((12,)),
    ]
    shapes = [
        (edges, width),
        (edges, width),
        (depth, width * rows),
        (1, width * rows),
        w_basis.shape,
    ]
    specs = [pl.BlockSpec(memory_space=pltpu.VMEM)]
    out, grad_out, layer_share, rev_share, grad_basis = pl.pallas_call(
        lambda *refs: block_kernel(devices, scale, *refs),
        out_shape=[jax.ShapeDtypeStruct(shape, F32) for shape in shapes],
        in_specs=specs * 11,
        out_specs=specs * 5,
        scratch_shapes=scratch,
        compiler_params=pltpu.CompilerParams(
            vmem_limit_bytes=VMEM_LIMIT, collective_id=0, has_side_effects=True
        ),
        name="block",
    )(
        messages,
        src_col,
        src_row,
        tgt_col,
        tgt_row,
        slot_col,
        tri_basis,
        w_basis,
        w_rev,
        w_layers,
        cotangent,
    )
    return (out, grad_out, layer_share, rev_share.reshape(-1), grad_basis)


def solution(mesh):
    in_specs = (
        P("edges", None),
        P("edges"),
        P(None, "edges"),
        P("edges"),
        P("edges"),
        P("edges"),
        P("edges"),
        P(),
        P(),
        P(),
        P("edges", None),
    )
    out_specs = (P("edges", None), P("edges", None), P(None, "edges"), P("edges"), P())
    return jax.shard_map(
        on_device, mesh=mesh, in_specs=in_specs, out_specs=out_specs, check_vma=False
    )
```

time: 192 us -> 73.8 us (0.38)
  waiting for transfers between devices: 84.7 us -> 0 us
  blocking collectives: 42.9 us -> 0 us
  Pallas kernels: 25.9 us -> 59.4 us
  between operations: 14.9 us -> 1.33 us
  starting transfers between devices: 11.4 us -> 0 us
    reduce_scatter x1 -> x0, waiting for transfers between devices: 73.8 us -> none  [on_device(): lax.psum_scatter(weight_grads, 'edges', scatter_dimension=1, tiled=True)]
    psum x1 -> x0, blocking collectives: 42.9 us -> none  [on_device(): grad_basis = lax.psum(basis_grad, 'edges')]
    pallas_call x4 -> x1, Pallas kernels: 25.9 us -> 59.4 us  [on_device(): pl.pallas_call(lambda *refs: block_kernel(devices, scale, *refs), out_sha...]
    ppermute x12 -> x0, starting transfers between devices: 11.4 us -> none  [the longest x4 9.89 us: shift(): lax.ppermute(block, 'edges', [(i, (i + distance) % count) for i in range(...]
    ppermute x12 -> x0, waiting for transfers between devices: 10.9 us -> none  [the longest x4 9.41 us: shift(): lax.ppermute(block, 'edges', [(i, (i + distance) % count) for i in range(...]
    slice x3 -> x0, local copies, waits for them, and re-layouts: 2.96 us -> none  [the longest x2 2.26 us: exchange(): rows[k * group:(k + 1) * group]]
    unnamed x34 -> x13, local copies, waits for them, and re-layouts: 7.4 us -> 4.89 us
  transfers between devices with their start and end apart: 13 -> 0, of which waited for: 4 -> 0; matrix products, arithmetic and copies ran while one was open for 2% -> 0% of each run, Pallas kernels for 8% -> 0%
where the time goes in v3:
time: 73.8 us; the launch traced here: 73.4 us
  Pallas kernels  59.4 us (80%)
  local copies, waits for them, and re-layouts  11.3 us (15%)
  other arithmetic  1.43 us (2%)
  between operations  1.33 us (2%)
    pallas_call x1, Pallas kernels, on_device(): pl.pallas_call(lambda *refs: block_kernel(devices, scale, *refs), out_sha...  59.4 us
    unnamed x13, local copies, waits for them, and re-layouts  4.89 us
    reshape x1, local copies, waits for them, and re-layouts, on_device(): tri_source.reshape(slots, 1)  1.84 us
    select_n x2, local copies, waits for them, and re-layouts, on_device(): target = jnp.where(live[:, None], target, -1)  1.75 us
    reshape x1, local copies, waits for them, and re-layouts, on_device(): slot_col = rev_slot.reshape(edges, 1)  1.48 us

profile of v3, /device:TPU:0, one launch (start us, length us, event | category | flops | bytes accessed | tf_op | source)
XLA Modules:
  0.0 73.4 jit_solution(8630716834688987205)
XLA Ops:
  1.3 0.7 broadcast_multiply_fusion
  1.9 1.3 %reshape.54.refs_2_ = s32[1,1536]{1,0:T(1,128)} reshape(s32[1536]{0:T(1024)} %param.14) | data formatting | bytes 12288 | tf_op jit(solution)/shard_map/reshape | solution.py:371
  3.2 0.8 %fusion = s32[1536]{0:T(1024)S(1)} fusion(s32[1536]{0:T(1024)} %param.15, s32[12]{0:T(128)S(1)} %broadcast_multiply_fusion, pred[12]{0:T(512)(128)(4,1)S(1)} %iota_compare_fusion), kind=kLoop, calls=%fused_computation.1 | loop fusion | flops 3072 | bytes 12348 | tf_op jit(solution)/shard_map/jit(_where)/select_n | solution.py:369
  4.0 0.6 select_n.14.refs_4_
  4.6 1.5 %reshape.58.refs_5_ = s32[384,1]{1,0:T(8,128)} reshape(s32[384]{0:T(512)} %param.12) | data formatting | bytes 3072 | tf_op jit(solution)/shard_map/reshape | solution.py:372
  6.1 1.1 %select_n.15.refs_3_ = s32[1536,1]{1,0:T(8,128)} reshape(s32[1536]{0:T(1024)S(1)} %fusion) | data formatting | bytes 12288 | tf_op jit(solution)/shard_map/jit(_where)/select_n | solution.py:369
  7.2 1.8 %reshape.57.refs_1_ = s32[1536,1]{1,0:T(8,128)} reshape(s32[1536]{0:T(1024)} %param.14) | data formatting | bytes 12288 | tf_op jit(solution)/shard_map/reshape | solution.py:371
  9.1 59.4 %block.1 = (f32[384,512]{1,0:T(8,128)}, f32[384,512]{1,0:T(8,128)}, f32[2,8192]{1,0:T(2,128)}, f32[1,8192]{1,0:T(1,128)}, f32[16,512]{1,0:T(8,128)}) custom-call(f32[384,512]{1,0:T(8,128)} %refs_0_.1, s32[1536,1]{1,0:T(8,128)} %reshape.57.refs_1_, s32[1,1536]{1,0:T(1,128)} %reshape.54.refs_2_, s32[1536,1]{1,0:T(8,128)} %select_n.15.refs_3_, ...), custom_call_target="tpu_custom_call" | custom-call | tf_op jit(solution)/shard_map/block/pallas_call | solution.py:403
  68.5 0.0 copy-start
  68.5 0.0 copy-start.1
  68.5 0.0 copy-start.3
  68.5 0.0 copy-start.2
  68.5 2.1 %copy.25 = f32[384,512]{1,0:T(8,128)} copy(f32[384,512]{1,0:T(8,128)} %get-tuple-element.20) | data formatting | bytes 1572864
  70.6 0.0 copy-done
  70.6 0.9 %copy.26 = f32[384,512]{1,0:T(8,128)} copy(f32[384,512]{1,0:T(8,128)S(1)} %copy-done) | data formatting | bytes 1572864
  71.5 0.0 copy-done.1
  71.5 0.6 copy.27
  72.2 0.0 copy-done.3
  72.2 0.6 copy.28
  72.8 0.0 copy-done.2
  72.8 0.6 copy.29
  (1 shorter events, 0.0 us)
Async XLA Ops:
  68.5 2.2 %copy-start = (f32[384,512]{1,0:T(8,128)S(1)}, f32[384,512]{1,0:T(8,128)}, u32[]{:S(2)}) copy-start(f32[384,512]{1,0:T(8,128)} %get-tuple-element.21) | copy-start | bytes 2359300
  68.5 3.0 %copy-start.1 = (f32[2,8192]{1,0:T(2,128)S(1)}, f32[2,8192]{1,0:T(2,128)}, u32[]{:S(2)}) copy-start(f32[2,8192]{1,0:T(2,128)} %get-tuple-element.22) | copy-start | bytes 196612
  68.5 3.7 %copy-start.3 = (f32[1,8192]{1,0:T(1,128)S(1)}, f32[1,8192]{1,0:T(1,128)}, u32[]{:S(2)}) copy-start(f32[1,8192]{1,0:T(1,128)} %get-tuple-element.13) | copy-start | bytes 98308
  68.5 4.3 %copy-start.2 = (f32[16,512]{1,0:T(8,128)S(1)}, f32[16,512]{1,0:T(8,128)}, u32[]{:S(2)}) copy-start(f32[16,512]{1,0:T(8,128)} %get-tuple-element.24) | copy-start | bytes 98308

commit v4 on v3

--- a/solution.py
+++ b/solution.py
@@ -33,6 +33,10 @@
 def onehot_rows(column, width):
     ids = lax.broadcasted_iota(jnp.int32, (column.shape[0], width), 1)
     return jnp.where(column == ids, 1.0, 0.0).astype(BF16)
+
+
+def column_of(row):
+    return jnp.broadcast_to(row, (8, row.shape[1])).T[:, :1]
 
 
 def onehot_columns(row, height):
@@ -147,11 +151,9 @@
     devices,
     scale,
     messages,
-    src_col,
     src_row,
-    tgt_col,
     tgt_row,
-    slot_col,
+    slot_row,
     basis,
     w_basis,
     w_rev,
@@ -221,13 +223,15 @@
         return jnp.concatenate(highs, axis=0), jnp.concatenate(lows, axis=0)
 
     forth = exchange(messages, arrived, 2)
+    src_col, tgt_col = column_of(src_row[...]), column_of(tgt_row[...])
+    slot_col = column_of(slot_row[...])
     window[halo : halo + edges, :] = messages[...]
     tri_weight[...] = triplet_weight(basis[...], w_basis[...])
     weights = [split(w_layers[layer]) for layer in range(depth)]
     weight_rev = split(w_rev[...])
     for copy in halos:
         copy.wait_recv()
-    gathered[...] = pick(onehot_rows(src_col[...], edges + 2 * halo), window[...])
+    gathered[...] = pick(onehot_rows(src_col, edges + 2 * halo), window[...])
     agg = pick(onehot_columns(tgt_row[...], edges), gathered[...] * tri_weight[...])
 
     rev = collect(forth, arrived)
@@ -274,7 +278,7 @@
     spread(parts, depth, dot3(rev, split(g_rev_rows), ((0,), (0,))) * scale)
     advance(depth)
     advance(0)
-    grad_prod = pick(onehot_rows(tgt_col[...], edges), grad)
+    grad_prod = pick(onehot_rows(tgt_col, edges), grad)
     basis_sum[0] = dot3(split(basis[...]), split(grad_prod * gathered[...])) * scale
     last = len(chains)
     basis_copies = []
@@ -367,9 +371,9 @@
     live = jnp.arange(tiles, dtype=jnp.int32) < tile_count[0]
     target = tile_block[:, None] * 128 + tri_target.reshape(tiles, 128)
     target = jnp.where(live[:, None], target, -1)
-    tgt_row, tgt_col = target.reshape(1, slots), target.reshape(slots, 1)
-    src_row, src_col = tri_source.reshape(1, slots), tri_source.reshape(slots, 1)
-    slot_col = rev_slot.reshape(edges, 1)
+    tgt_row = target.reshape(1, slots)
+    src_row = tri_source.reshape(1, slots)
+    slot_row = rev_slot.reshape(1, edges)
 
     rows, half, chains = width // devices, width // 2, 2 * (depth + 1)
     sizes = [devices >> (step + 1) for step in range(levels)]
@@ -403,7 +407,7 @@
     out, grad_out, layer_share, rev_share, grad_basis = pl.pallas_call(
         lambda *refs: block_kernel(devices, scale, *refs),
         out_shape=[jax.ShapeDtypeStruct(shape, F32) for shape in shapes],
-        in_specs=specs * 11,
+        in_specs=specs * 9,
         out_specs=specs * 5,
         scratch_shapes=scratch,
         compiler_params=pltpu.CompilerParams(
@@ -412,11 +416,9 @@
         name="block",
     )(
         messages,
-        src_col,
         src_row,
-        tgt_col,
         tgt_row,
-        slot_col,
+        slot_row,
         tri_basis,
         w_basis,
         w_rev,

time: 73.8 us -> 70.2 us (0.951)
  local copies, waits for them, and re-layouts: 11.3 us -> 8.03 us
    reshape x3 -> x2, local copies, waits for them, and re-layouts: 4.62 us -> 2.54 us  [the longest x1 1.29 us: on_device(): src_row = tri_source.reshape(1, slots)]
    select_n x2 -> x1, local copies, waits for them, and re-layouts: 1.75 us -> 0.6 us  [on_device(): target = jnp.where(live[:, None], target, -1)]
where the time goes in v4:
time: 70.2 us; the launch traced here: 69.9 us
  Pallas kernels  59.1 us (84%)
  local copies, waits for them, and re-layouts  8.03 us (11%)
  other arithmetic  1.43 us (2%)
  between operations  1.33 us (2%)
    pallas_call x1, Pallas kernels, on_device(): pl.pallas_call(lambda *refs: block_kernel(devices, scale, *refs), out_sha...  59.1 us
    unnamed x13, local copies, waits for them, and re-layouts  4.89 us

profile of v4, /device:TPU:0, one launch (start us, length us, event | category | flops | bytes accessed | tf_op | source)
XLA Modules:
  0.0 69.9 jit_solution(2970758029217336509)
XLA Ops:
  1.3 0.7 broadcast_multiply_fusion
  1.9 1.2 %reshape.39.refs_3_ = s32[1,384]{1,0:T(1,128)} reshape(s32[384]{0:T(512)} %param.12) | data formatting | bytes 3072 | tf_op jit(solution)/shard_map/reshape | solution.py:376
  3.2 1.3 %reshape.38.refs_1_ = s32[1,1536]{1,0:T(1,128)} reshape(s32[1536]{0:T(1024)} %param.14) | data formatting | bytes 12288 | tf_op jit(solution)/shard_map/reshape | solution.py:375
  4.5 0.8 %fusion = s32[1536]{0:T(1024)S(1)} fusion(s32[1536]{0:T(1024)} %param.15, s32[12]{0:T(128)S(1)} %broadcast_multiply_fusion, pred[12]{0:T(512)(128)(4,1)S(1)} %iota_compare_fusion), kind=kLoop, calls=%fused_computation.1 | loop fusion | flops 3072 | bytes 12348 | tf_op jit(solution)/shard_map/jit(_where)/select_n | solution.py:373
  5.3 0.6 select_n.9.refs_2_
  5.9 59.1 %block.1 = (f32[384,512]{1,0:T(8,128)}, f32[384,512]{1,0:T(8,128)}, f32[2,8192]{1,0:T(2,128)}, f32[1,8192]{1,0:T(1,128)}, f32[16,512]{1,0:T(8,128)}) custom-call(f32[384,512]{1,0:T(8,128)} %refs_0_.1, s32[1,1536]{1,0:T(1,128)} %reshape.38.refs_1_, s32[1,1536]{1,0:T(1,128)} %select_n.9.refs_2_, s32[1,384]{1,0:T(1,128)} %reshape.39.refs_3_, ...), custom_call_target="tpu_custom_call" | custom-call | tf_op jit(solution)/shard_map/block/pallas_call | solution.py:407
  65.0 0.0 copy-start
  65.0 0.0 copy-start.1
  65.0 0.0 copy-start.3
  65.0 0.0 copy-start.2
  65.0 2.1 %copy.22 = f32[384,512]{1,0:T(8,128)} copy(f32[384,512]{1,0:T(8,128)} %get-tuple-element.20) | data formatting | bytes 1572864
  67.1 0.0 copy-done
  67.1 0.9 %copy.23 = f32[384,512]{1,0:T(8,128)} copy(f32[384,512]{1,0:T(8,128)S(1)} %copy-done) | data formatting | bytes 1572864
  68.0 0.0 copy-done.1
  68.0 0.6 copy.24
  68.6 0.0 copy-done.3
  68.6 0.6 copy.25
  69.3 0.0 copy-done.2
  69.3 0.6 copy.26
  (1 shorter events, 0.0 us)
Async XLA Ops:
  65.0 2.2 %copy-start = (f32[384,512]{1,0:T(8,128)S(1)}, f32[384,512]{1,0:T(8,128)}, u32[]{:S(2)}) copy-start(f32[384,512]{1,0:T(8,128)} %get-tuple-element.21) | copy-start | bytes 2359300
  65.0 3.0 %copy-start.1 = (f32[2,8192]{1,0:T(2,128)S(1)}, f32[2,8192]{1,0:T(2,128)}, u32[]{:S(2)}) copy-start(f32[2,8192]{1,0:T(2,128)} %get-tuple-element.22) | copy-start | bytes 196612
  65.0 3.7 %copy-start.3 = (f32[1,8192]{1,0:T(1,128)S(1)}, f32[1,8192]{1,0:T(1,128)}, u32[]{:S(2)}) copy-start(f32[1,8192]{1,0:T(1,128)} %get-tuple-element.13) | copy-start | bytes 98308
  65.0 4.3 %copy-start.2 = (f32[16,512]{1,0:T(8,128)S(1)}, f32[16,512]{1,0:T(8,128)}, u32[]{:S(2)}) copy-start(f32[16,512]{1,0:T(8,128)} %get-tuple-element.24) | copy-start | bytes 98308

commit v5 on v4

--- a/solution.py
+++ b/solution.py
@@ -151,9 +151,7 @@
     devices,
     scale,
     messages,
-    src_row,
-    tgt_row,
-    slot_row,
+    index_row,
     basis,
     w_basis,
     w_rev,
@@ -204,17 +202,17 @@
         ),
     ]
 
-    def exchange(rows, target, first):
-        copies = [None] * 4
-        for k in (3, 2, 1, 0):
+    def exchange(rows, target, first, groups):
+        copies = {}
+        for k in reversed(groups):
             copies[k] = row_copy(
                 rows.at[pl.ds(k * group, group)], target.at[k], first + k, me ^ (1 << bits[k])
             )
         return copies
 
-    def collect(copies, target):
+    def collect(copies, target, groups):
         highs, lows = [], []
-        for k in range(4):
+        for k in groups:
             onehot = onehot_rows(slot_col[k * group : (k + 1) * group, :], group)
             copies[k].wait_recv()
             ah, al = split(target[k])
@@ -222,9 +220,11 @@
             lows.append(dot(onehot, al).astype(BF16))
         return jnp.concatenate(highs, axis=0), jnp.concatenate(lows, axis=0)
 
-    forth = exchange(messages, arrived, 2)
-    src_col, tgt_col = column_of(src_row[...]), column_of(tgt_row[...])
-    slot_col = column_of(slot_row[...])
+    forth = exchange(messages, arrived, 2, range(4))
+    slots = basis.shape[1]
+    src_row, tgt_row = index_row[:, :slots], index_row[:, slots : 2 * slots]
+    src_col, tgt_col = column_of(src_row), column_of(tgt_row)
+    slot_col = column_of(index_row[:, 2 * slots :])
     window[halo : halo + edges, :] = messages[...]
     tri_weight[...] = triplet_weight(basis[...], w_basis[...])
     weights = [split(w_layers[layer]) for layer in range(depth)]
@@ -232,28 +232,46 @@
     for copy in halos:
         copy.wait_recv()
     gathered[...] = pick(onehot_rows(src_col, edges + 2 * halo), window[...])
-    agg = pick(onehot_columns(tgt_row[...], edges), gathered[...] * tri_weight[...])
-
-    rev = collect(forth, arrived)
-    gate, rev_slope = silu_pair(dot3(rev, weight_rev))
-    msg = messages[...]
-    hidden = msg + agg + msg * gate
-    states, slopes, grad_pres = [], [], [None] * depth
-    for layer in range(depth):
-        state = split(hidden)
-        act, slope = silu_pair(dot3(state, weights[layer]))
-        hidden = hidden + act
-        states.append(state)
-        slopes.append(slope)
-    out[...] = hidden
-    grad = cotangent[...]
+    agg = pick(onehot_columns(tgt_row, edges), gathered[...] * tri_weight[...])
+
+    def forward(groups):
+        start, stop = groups[0] * group, (groups[-1] + 1) * group
+        rev = collect(forth, arrived, groups)
+        gate, rev_slope = silu_pair(dot3(rev, weight_rev))
+        msg = messages[start:stop, :]
+        hidden = msg + agg[start:stop, :] + msg * gate
+        states, slopes = [], []
+        for layer in range(depth):
+            state = split(hidden)
+            act, slope = silu_pair(dot3(state, weights[layer]))
+            hidden = hidden + act
+            states.append(state)
+            slopes.append(slope)
+        out[start:stop, :] = hidden
+        return start, stop, rev, gate, rev_slope, states, slopes
+
+    def step_back(grad, slope, weight):
+        grad_pre = split(grad * slope)
+        return grad_pre, grad + dot3(grad_pre, weight, ((1,), (1,)))
+
+    def leave(done, grad, groups):
+        start, stop, _, gate, rev_slope, _, _ = done
+        g_rev[start:stop, :] = grad * messages[start:stop, :] * rev_slope
+        grad_out[start:stop, :] = grad * (1.0 + gate)
+        return exchange(g_rev, returned, 6, groups)
+
+    def joined(first, second):
+        return tuple(jnp.concatenate(pair, axis=0) for pair in zip(first, second))
+
+    early, late = range(0, 2), range(2, 4)
+    done_a = forward(early)
+    grad_a = cotangent[done_a[0] : done_a[1], :]
+    pres_a = [None] * depth
     for layer in range(depth - 1, -1, -1):
-        grad_pres[layer] = split(grad * slopes[layer])
-        grad = grad + dot3(grad_pres[layer], weights[layer], ((1,), (1,)))
-    g_rev_rows = grad * msg * rev_slope
-    g_rev[...] = g_rev_rows
-    back = exchange(g_rev, returned, 6)
-    grad_out[...] = grad * (1.0 + gate)
+        pres_a[layer], grad_a = step_back(grad_a, done_a[6][layer], weights[layer])
+    back = leave(done_a, grad_a, early)
+    done_b = forward(late)
+    grad_b = cotangent[done_b[0] : done_b[1], :]
 
     orders = routes(devices)
     chains = []
@@ -271,11 +289,17 @@
         chains[2 * m + 1].advance()
 
     for layer in range(depth - 1, -1, -1):
-        product = dot3(states[layer], grad_pres[layer], ((0,), (0,)))
+        pre, grad_b = step_back(grad_b, done_b[6][layer], weights[layer])
+        if layer == 0:
+            back.update(leave(done_b, grad_b, late))
+        state = joined(done_a[5][layer], done_b[5][layer])
+        product = dot3(state, joined(pres_a[layer], pre), ((0,), (0,)))
         spread(parts, layer, product * scale)
         for m in range(depth - 1, layer - 1, -1):
             advance(m)
-    spread(parts, depth, dot3(rev, split(g_rev_rows), ((0,), (0,))) * scale)
+    grad = jnp.concatenate([grad_a, grad_b], axis=0)
+    rev = joined(done_a[2], done_b[2])
+    spread(parts, depth, dot3(rev, split(g_rev[...]), ((0,), (0,))) * scale)
     advance(depth)
     advance(0)
     grad_prod = pick(onehot_rows(tgt_col, edges), grad)
@@ -302,7 +326,7 @@
     basis_advance()
     advance(depth)
     window_grad[...] = pick(
-        onehot_columns(src_row[...], edges + 2 * halo), grad_prod * tri_weight[...]
+        onehot_columns(src_row, edges + 2 * halo), grad_prod * tri_weight[...]
     )
     rim_copies = [
         row_copy(window_grad.at[pl.ds(0, halo)], rims.at[0], 10, behind),
@@ -314,7 +338,7 @@
     grad_out[...] = (
         grad_out[...]
         + window_grad[halo : halo + edges, :]
-        + dot3(collect(back, returned), weight_rev, ((1,), (1,)))
+        + dot3(collect(back, returned, range(4)), weight_rev, ((1,), (1,)))
     )
     advance(depth)
     for step in range(2, levels):
@@ -339,7 +363,7 @@
                 rev_out[0:1, spot] = total[0, row : row + 1, :]
     basis_advance()
     basis_out[...] = basis_sum[levels]
-    for copy in halos + forth + back + rim_copies + basis_copies:
+    for copy in halos + list(forth.values()) + list(back.values()) + rim_copies + basis_copies:
         copy.wait_send()
     for chain in chains:
         for copy in chain.copies:
@@ -371,9 +395,7 @@
     live = jnp.arange(tiles, dtype=jnp.int32) < tile_count[0]
     target = tile_block[:, None] * 128 + tri_target.reshape(tiles, 128)
     target = jnp.where(live[:, None], target, -1)
-    tgt_row = target.reshape(1, slots)
-    src_row = tri_source.reshape(1, slots)
-    slot_row = rev_slot.reshape(1, edges)
+    index_row = jnp.concatenate([tri_source, target.reshape(slots), rev_slot]).reshape(1, -1)
 
     rows, half, chains = width // devices, width // 2, 2 * (depth + 1)
     sizes = [devices >> (step + 1) for step in range(levels)]
@@ -407,7 +429,7 @@
     out, grad_out, layer_share, rev_share, grad_basis = pl.pallas_call(
         lambda *refs: block_kernel(devices, scale, *refs),
         out_shape=[jax.ShapeDtypeStruct(shape, F32) for shape in shapes],
-        in_specs=specs * 9,
+        in_specs=specs * 7,
         out_specs=specs * 5,
         scratch_shapes=scratch,
         compiler_params=pltpu.CompilerParams(
@@ -416,9 +438,7 @@
         name="block",
     )(
         messages,
-        src_row,
-        tgt_row,
-        slot_row,
+        index_row,
         tri_basis,
         w_basis,
         w_rev,

time: 70.2 us -> 69 us (0.983)
  the two profiles are of different devices: /device:TPU:0 before, /device:TPU:4 now
where the time goes in v5:
time: 69 us; the launch traced here: 68.7 us
  Pallas kernels  59.7 us (87%)
  local copies, waits for them, and re-layouts  5.5 us (8%)
  other arithmetic  2.16 us (3%)
  between operations  1.33 us (2%)
    pallas_call x1, Pallas kernels, on_device(): pl.pallas_call(lambda *refs: block_kernel(devices, scale, *refs), out_sha...  59.7 us
    unnamed x13, local copies, waits for them, and re-layouts  4.89 us

profile of v5, /device:TPU:4, one launch (start us, length us, event | category | flops | bytes accessed | tf_op | source)
XLA Modules:
  0.0 68.7 jit_solution(743687767410810374)
XLA Ops:
  1.3 0.7 broadcast_multiply_fusion
  1.9 0.8 %fusion = s32[1536]{0:T(1024)S(1)} fusion(s32[1536]{0:T(1024)} %param.15, s32[12]{0:T(128)S(1)} %broadcast_multiply_fusion, pred[12]{0:T(512)(128)(4,1)S(1)} %iota_compare_fusion), kind=kLoop, calls=%fused_computation.2 | loop fusion | flops 3072 | bytes 12348 | tf_op jit(solution)/shard_map/jit(_where)/select_n | solution.py:397
  2.7 0.7 %pad_add_fusion = s32[3456]{0:T(1024)S(1)} fusion(s32[384]{0:T(512)} %param.12, s32[1536]{0:T(1024)S(1)} %fusion, s32[1536]{0:T(1024)} %param.14), kind=kLoop, calls=%fused_computation | loop fusion | flops 6912 | bytes 27648 | tf_op jit(solution)/shard_map/concatenate | solution.py:398
  3.4 0.6 reshape.26.refs_1_
  4.1 59.7 %block.1 = (f32[384,512]{1,0:T(8,128)}, f32[384,512]{1,0:T(8,128)}, f32[2,8192]{1,0:T(2,128)}, f32[1,8192]{1,0:T(1,128)}, f32[16,512]{1,0:T(8,128)}) custom-call(f32[384,512]{1,0:T(8,128)} %refs_0_.1, s32[1,3456]{1,0:T(1,128)} %reshape.26.refs_1_, f32[16,1536]{1,0:T(8,128)} %refs_2_.1, f32[16,512]{1,0:T(8,128)} %refs_3_.1, f32[512,512]{1,0:T(8,128)} %refs_4_.1, ...), custom_call_target="tpu_custom_call" | custom-call | tf_op jit(solution)/shard_map/block/pallas_call | solution.py:429
  63.8 0.0 copy-start
  63.8 0.0 copy-start.1
  63.8 0.0 copy-start.3
  63.8 0.0 copy-start.2
  63.8 2.1 %copy.22 = f32[384,512]{1,0:T(8,128)} copy(f32[384,512]{1,0:T(8,128)} %get-tuple-element.20) | data formatting | bytes 1572864
  65.9 0.0 copy-done
  65.9 0.9 %copy.23 = f32[384,512]{1,0:T(8,128)} copy(f32[384,512]{1,0:T(8,128)S(1)} %copy-done) | data formatting | bytes 1572864
  66.8 0.0 copy-done.1
  66.8 0.6 copy.24
  67.4 0.0 copy-done.3
  67.5 0.6 copy.25
  68.1 0.0 copy-done.2
  68.1 0.6 copy.26
  (1 shorter events, 0.0 us)
Async XLA Ops:
  63.8 2.2 %copy-start = (f32[384,512]{1,0:T(8,128)S(1)}, f32[384,512]{1,0:T(8,128)}, u32[]{:S(2)}) copy-start(f32[384,512]{1,0:T(8,128)} %get-tuple-element.21) | copy-start | bytes 2359300
  63.8 3.0 %copy-start.1 = (f32[2,8192]{1,0:T(2,128)S(1)}, f32[2,8192]{1,0:T(2,128)}, u32[]{:S(2)}) copy-start(f32[2,8192]{1,0:T(2,128)} %get-tuple-element.22) | copy-start | bytes 196612
  63.8 3.7 %copy-start.3 = (f32[1,8192]{1,0:T(1,128)S(1)}, f32[1,8192]{1,0:T(1,128)}, u32[]{:S(2)}) copy-start(f32[1,8192]{1,0:T(1,128)} %get-tuple-element.13) | copy-start | bytes 98308
  63.8 4.3 %copy-start.2 = (f32[16,512]{1,0:T(8,128)S(1)}, f32[16,512]{1,0:T(8,128)}, u32[]{:S(2)}) copy-start(f32[16,512]{1,0:T(8,128)} %get-tuple-element.24) | copy-start | bytes 98308

commit v6 on v5

--- a/solution.py
+++ b/solution.py
@@ -324,6 +324,7 @@
             )
 
     basis_advance()
+    advance(depth - 1)
     advance(depth)
     window_grad[...] = pick(
         onehot_columns(src_row, edges + 2 * halo), grad_prod * tri_weight[...]
@@ -335,13 +336,13 @@
     for m in range(depth - 1, -1, -1):
         advance(m)
     basis_advance()
-    grad_out[...] = (
-        grad_out[...]
-        + window_grad[halo : halo + edges, :]
-        + dot3(collect(back, returned, range(4)), weight_rev, ((1,), (1,)))
-    )
-    advance(depth)
     for step in range(2, levels):
+        if step == levels - 1:
+            grad_out[...] = (
+                grad_out[...]
+                + window_grad[halo : halo + edges, :]
+                + dot3(collect(back, returned, range(4)), weight_rev, ((1,), (1,)))
+            )
         for m in list(range(depth - 1, -1, -1)) + [depth]:
             advance(m)
         basis_advance()

time: 69 us -> 69 us (level)
  the two profiles are of different devices: /device:TPU:4 before, /device:TPU:0 now
where the time goes in v6:
time: 69 us; the launch traced here: 68.7 us
  Pallas kernels  59.7 us (87%)
  local copies, waits for them, and re-layouts  5.5 us (8%)
  other arithmetic  2.16 us (3%)
  between operations  1.33 us (2%)
    pallas_call x1, Pallas kernels, on_device(): pl.pallas_call(lambda *refs: block_kernel(devices, scale, *refs), out_sha...  59.7 us
    unnamed x13, local copies, waits for them, and re-layouts  4.89 us

profile of v6, /device:TPU:0, one launch (start us, length us, event | category | flops | bytes accessed | tf_op | source)
XLA Modules:
  0.0 68.7 jit_solution(14409159208398794739)
XLA Ops:
  1.3 0.7 broadcast_multiply_fusion
  1.9 0.8 %fusion = s32[1536]{0:T(1024)S(1)} fusion(s32[1536]{0:T(1024)} %param.15, s32[12]{0:T(128)S(1)} %broadcast_multiply_fusion, pred[12]{0:T(512)(128)(4,1)S(1)} %iota_compare_fusion), kind=kLoop, calls=%fused_computation.2 | loop fusion | flops 3072 | bytes 12348 | tf_op jit(solution)/shard_map/jit(_where)/select_n | solution.py:398
  2.7 0.7 %pad_add_fusion = s32[3456]{0:T(1024)S(1)} fusion(s32[384]{0:T(512)} %param.12, s32[1536]{0:T(1024)S(1)} %fusion, s32[1536]{0:T(1024)} %param.14), kind=kLoop, calls=%fused_computation | loop fusion | flops 6912 | bytes 27648 | tf_op jit(solution)/shard_map/concatenate | solution.py:399
  3.4 0.6 reshape.26.refs_1_
  4.1 59.7 %block.1 = (f32[384,512]{1,0:T(8,128)}, f32[384,512]{1,0:T(8,128)}, f32[2,8192]{1,0:T(2,128)}, f32[1,8192]{1,0:T(1,128)}, f32[16,512]{1,0:T(8,128)}) custom-call(f32[384,512]{1,0:T(8,128)} %refs_0_.1, s32[1,3456]{1,0:T(1,128)} %reshape.26.refs_1_, f32[16,1536]{1,0:T(8,128)} %refs_2_.1, f32[16,512]{1,0:T(8,128)} %refs_3_.1, f32[512,512]{1,0:T(8,128)} %refs_4_.1, ...), custom_call_target="tpu_custom_call" | custom-call | tf_op jit(solution)/shard_map/block/pallas_call | solution.py:430
  63.8 0.0 copy-start
  63.8 0.0 copy-start.1
  63.8 0.0 copy-start.3
  63.8 0.0 copy-start.2
  63.8 2.1 %copy.22 = f32[384,512]{1,0:T(8,128)} copy(f32[384,512]{1,0:T(8,128)} %get-tuple-element.20) | data formatting | bytes 1572864
  66.0 0.0 copy-done
  66.0 0.9 %copy.23 = f32[384,512]{1,0:T(8,128)} copy(f32[384,512]{1,0:T(8,128)S(1)} %copy-done) | data formatting | bytes 1572864
  66.8 0.0 copy-done.1
  66.8 0.6 copy.24
  67.5 0.0 copy-done.3
  67.5 0.6 copy.25
  68.1 0.0 copy-done.2
  68.1 0.6 copy.26
  (1 shorter events, 0.0 us)
Async XLA Ops:
  63.8 2.2 %copy-start = (f32[384,512]{1,0:T(8,128)S(1)}, f32[384,512]{1,0:T(8,128)}, u32[]{:S(2)}) copy-start(f32[384,512]{1,0:T(8,128)} %get-tuple-element.21) | copy-start | bytes 2359300
  63.8 3.0 %copy-start.1 = (f32[2,8192]{1,0:T(2,128)S(1)}, f32[2,8192]{1,0:T(2,128)}, u32[]{:S(2)}) copy-start(f32[2,8192]{1,0:T(2,128)} %get-tuple-element.22) | copy-start | bytes 196612
  63.8 3.7 %copy-start.3 = (f32[1,8192]{1,0:T(1,128)S(1)}, f32[1,8192]{1,0:T(1,128)}, u32[]{:S(2)}) copy-start(f32[1,8192]{1,0:T(1,128)} %get-tuple-element.13) | copy-start | bytes 98308
  63.8 4.3 %copy-start.2 = (f32[16,512]{1,0:T(8,128)S(1)}, f32[16,512]{1,0:T(8,128)}, u32[]{:S(2)}) copy-start(f32[16,512]{1,0:T(8,128)} %get-tuple-element.24) | copy-start | bytes 98308
